TPU v7x, 32 devices: a whole 2x2x4 slice. The times are simulated.
32 devices in a mesh: dp: 16 (over z, y, core), roi: 2 (over x).
Axes of the slice: x: 2, y: 2, z: 4, core: 2. Of those that a mesh axis runs over, the one named last changes fastest.
Arguments:
- feature_maps: bfloat16 [64, 1360, 256], P('dp'), may hold values from -6 to 6
- region_boxes: float32 [9216, 4], P(('dp', 'roi')), may hold values from 0 to 1, as said below
- levels: int32 [9216], P(('dp', 'roi')), may hold values from 0 to 3
- labels: int32 [9216], P(('dp', 'roi')), may hold values from 0 to 80
- image_of_roi: int32 [9216], P(('dp', 'roi')), may hold values from 0 to 63, as said below
- targets: int32 [9216, 4], P(('dp', 'roi')), may hold values from -8192 to 8191
- first_weight: float32 [12544, 1024], P(('dp', 'roi')), may hold values from -0.0546875 to 0.0546875
- second_weight: float32 [1024, 1024], P(('dp', 'roi')), may hold values from -0.1875 to 0.1875
- head_weight: float32 [1024, 85], replicated, may hold values from -0.1875 to 0.1875
- biases: float32 [2133], replicated, may hold values from -1.2 to 1.2
- head_moment: float32 [1024, 85], replicated, as said below
- bias_moment: float32 [2133], replicated, as said below
- left_first: float32 [12544, 12544], P(('dp', 'roi')), as said below
- left_first_root: float32 [12544, 12544], P(('dp', 'roi')), as said below
- right_first: float32 [1024, 1024], P(('dp', 'roi')), as said below
- right_first_root: float32 [1024, 1024], P(('dp', 'roi')), as said below
- left_second: float32 [1024, 1024], P(('dp', 'roi')), as said below
- left_second_root: float32 [1024, 1024], P(('dp', 'roi')), as said below
- right_second: float32 [1024, 1024], P(('dp', 'roi')), as said below
- right_second_root: float32 [1024, 1024], P(('dp', 'roi')), as said below
Outputs:
- region_loss: float32 [9216], P(('dp', 'roi'))
- decoded_boxes: float32 [9216, 4], P(('dp', 'roi'))
- map_gradient: float32 [64, 1360, 256], P('dp', 'roi')
- first_gradient: float32 [12544, 1024], P(('dp', 'roi'))
- new_left_first: float32 [12544, 12544], P(('dp', 'roi'))
- new_right_first: float32 [1024, 1024], P(('dp', 'roi'))
- new_first_weight: float32 [12544, 1024], P(('dp', 'roi'))
- second_gradient: float32 [1024, 1024], P(('dp', 'roi'))
- new_left_second: float32 [1024, 1024], P(('dp', 'roi'))
- new_right_second: float32 [1024, 1024], P(('dp', 'roi'))
- new_second_weight: float32 [1024, 1024], P(('dp', 'roi'))
- head_gradient: float32 [1024, 85], replicated
- new_head_moment: float32 [1024, 85], replicated
- new_head_weight: float32 [1024, 85], replicated
- bias_gradient: float32 [2133], replicated
- new_bias_moment: float32 [2133], replicated
- new_biases: float32 [2133], replicated
Inputs may be any that keep to these rules, and one draw needn't show every extreme that they name: `image_of_roi`: every image has exactly 144 regions, and they lie in its group's rows: row r names an image of the group r // 576, that is from that group times 4 up to the next group's first image. `region_boxes`: x1 < x2 and y1 < y2. `left_first`: symmetric. `left_first_root`: symmetric. `right_first`: symmetric. `right_first_root`: symmetric. `left_second`: symmetric. `left_second_root`: symmetric. `right_second`: symmetric. `right_second_root`: symmetric. `head_moment`: positive. `bias_moment`: positive.
All inputs are finite; a program needn't handle non-finite values.
Results may differ from a plain program's by a relative error of at most 0.0055.
The roundings to bfloat16 on the way count: a program that leaves them out, or rounds other values in their place, can miss the bound.
Values may be sent and summed in bfloat16 or wider, within the bound.
A program may use at most 320 MiB of HBM per device.

v0:
```python
import jax
import jax.numpy as jnp
from jax import lax
from jax.sharding import PartitionSpec as P

POOL = 7
MAP = 32


BETA = 0.95
DECAY = 0.99
RATE_FIRST = 0.01
RATE_SECOND = 0.03
RATE_HEAD = 0.005
RATE_BIAS = 0.05
EPSILON = 1e-08
FIXED_POINT = 4096.0


def corner_plan(region_boxes, levels, top_side, pool_size):
    centers = (jnp.arange(pool_size, dtype=jnp.float32) + 0.5) / pool_size
    picked = levels[:, None] == jnp.arange(4, dtype=jnp.int32)[None, :]
    quarter = top_side * top_side
    side_table = jnp.array([top_side, top_side // 2, top_side // 4, top_side // 8], dtype=jnp.int32)
    start_table = jnp.array(
        [0, quarter, quarter + quarter // 4, quarter + quarter // 4 + quarter // 16],
        dtype=jnp.int32,
    )
    side_cells = jnp.sum(jnp.where(picked, side_table[None, :], 0), axis=1)
    level_start = jnp.sum(jnp.where(picked, start_table[None, :], 0), axis=1)
    side_float = side_cells.astype(jnp.float32)[:, None]
    across = region_boxes[:, 0:1] + centers[None, :] * (region_boxes[:, 2:3] - region_boxes[:, 0:1])
    downward = region_boxes[:, 1:2] + centers[None, :] * (
        region_boxes[:, 3:4] - region_boxes[:, 1:2]
    )
    across = jnp.clip(across * side_float - 0.5, 0.0, side_float - 1.0)
    downward = jnp.clip(downward * side_float - 0.5, 0.0, side_float - 1.0)
    left_col = jnp.floor(across).astype(jnp.int32)
    top_row = jnp.floor(downward).astype(jnp.int32)
    last_cell = side_cells[:, None] - 1
    right_col = jnp.minimum(left_col + 1, last_cell)
    bottom_row = jnp.minimum(top_row + 1, last_cell)
    frac_x = (across - left_col.astype(jnp.float32))[:, None, :]
    frac_y = (downward - top_row.astype(jnp.float32))[:, :, None]
    level_base = level_start[:, None, None]
    width_cells = side_cells[:, None, None]
    corner_cells = [
        level_base + top_row[:, :, None] * width_cells + left_col[:, None, :],
        level_base + top_row[:, :, None] * width_cells + right_col[:, None, :],
        level_base + bottom_row[:, :, None] * width_cells + left_col[:, None, :],
        level_base + bottom_row[:, :, None] * width_cells + right_col[:, None, :],
    ]
    corner_parts = [
        (1.0 - frac_y) * (1.0 - frac_x),
        (1.0 - frac_y) * frac_x,
        frac_y * (1.0 - frac_x),
        frac_y * frac_x,
    ]
    region_count = region_boxes.shape[0]
    cell_index = jnp.stack(corner_cells, axis=-1).reshape(region_count, pool_size * pool_size, 4)
    corner_weights = jnp.stack(corner_parts, axis=-1).reshape(
        region_count, pool_size * pool_size, 4
    )
    return (cell_index, corner_weights)


def decode_boxes(region_boxes, deltas):
    widths = region_boxes[:, 2] - region_boxes[:, 0]
    heights = region_boxes[:, 3] - region_boxes[:, 1]
    center_x = region_boxes[:, 0] + 0.5 * widths
    center_y = region_boxes[:, 1] + 0.5 * heights
    moved_x = center_x + deltas[:, 0] / 10.0 * widths
    moved_y = center_y + deltas[:, 1] / 10.0 * heights
    new_width = widths * jnp.exp(deltas[:, 2] / 5.0)
    new_height = heights * jnp.exp(deltas[:, 3] / 5.0)
    return jnp.stack(
        [
            moved_x - 0.5 * new_width,
            moved_y - 0.5 * new_height,
            moved_x + 0.5 * new_width,
            moved_y + 0.5 * new_height,
        ],
        axis=1,
    )


def huber_loss(residue):
    magnitude = jnp.abs(residue)
    return jnp.where(magnitude < 1.0, 0.5 * residue * residue, magnitude - 0.5)


def silu_slope(values):
    sigmoid = jax.nn.sigmoid(values)
    return sigmoid * (1.0 + values * (1.0 - sigmoid))


def rows_by_rows(left_side, right_side):
    return lax.dot_general(
        left_side, right_side, (((1,), (1,)), ((), ())), preferred_element_type=jnp.float32
    )


def cols_by_cols(left_side, right_side):
    return lax.dot_general(
        left_side, right_side, (((0,), (0,)), ((), ())), preferred_element_type=jnp.float32
    )


def shampoo_rows(
    rounded_rows,
    reduced_full,
    weight_rows,
    left_rows,
    left_root_rows,
    right_rows,
    right_root_full,
    step_rate,
    row_offset,
):
    new_left = BETA * left_rows + (1.0 - BETA) * rows_by_rows(rounded_rows, reduced_full)
    own_columns = lax.dynamic_slice_in_dim(reduced_full, row_offset, right_rows.shape[0], 1)
    new_right = BETA * right_rows + (1.0 - BETA) * cols_by_cols(own_columns, reduced_full)
    mixed = jnp.dot(
        left_root_rows.astype(jnp.bfloat16), reduced_full, preferred_element_type=jnp.float32
    )
    update = jnp.dot(mixed, right_root_full, precision=lax.Precision.HIGHEST)
    return (new_left, new_right, weight_rows - step_rate * update)


def diagonal_step(gradient, weight, moment, step_rate):
    new_moment = DECAY * moment + (1.0 - DECAY) * gradient * gradient
    return (new_moment, weight - step_rate * gradient / (jnp.sqrt(new_moment) + EPSILON))


def local(
    feature_maps,
    region_boxes,
    levels,
    labels,
    image_of_roi,
    targets,
    first_weight,
    second_weight,
    head_weight,
    biases,
    head_moment,
    bias_moment,
    left_first,
    left_first_root,
    right_first,
    right_first_root,
    left_second,
    left_second_root,
    right_second,
    right_second_root,
):
    region_count = region_boxes.shape[0]
    image_count = feature_maps.shape[0]
    cell_count = feature_maps.shape[1]
    channels = feature_maps.shape[2]
    hidden = head_weight.shape[0]
    classes = head_weight.shape[1] - 4
    loss_scale = 1.0 / (region_count * lax.axis_size("dp") * lax.axis_size("roi"))
    cell_index, corner_weights = corner_plan(region_boxes, levels, MAP, POOL)
    local_image = image_of_roi - lax.axis_index("dp") * image_count
    flat_rows = local_image[:, None, None] * cell_count + cell_index
    flat_maps = feature_maps.reshape(image_count * cell_count, channels)
    pooled = corner_weights[:, :, 0:1] * flat_maps[flat_rows[:, :, 0]]
    for corner in range(1, 4):
        pooled = (
            pooled + corner_weights[:, :, corner : corner + 1] * flat_maps[flat_rows[:, :, corner]]
        )
    pooled_low = pooled.reshape(region_count, -1).astype(jnp.bfloat16)
    first_low = first_weight.astype(jnp.bfloat16)
    second_low = second_weight.astype(jnp.bfloat16)
    head_low = head_weight.astype(jnp.bfloat16)
    bias_first = biases[:hidden]
    bias_second = biases[hidden : 2 * hidden]
    bias_head = biases[2 * hidden :]
    first_pre = (
        jnp.dot(
            pooled_low,
            lax.all_gather(first_low, ("dp", "roi"), axis=0, tiled=True),
            preferred_element_type=jnp.float32,
        )
        + bias_first
    )
    second_full = lax.all_gather(second_low, ("dp", "roi"), axis=0, tiled=True)
    first_act = jax.nn.silu(first_pre).astype(jnp.bfloat16)
    second_pre = jnp.dot(first_act, second_full, preferred_element_type=jnp.float32) + bias_second
    second_act = jax.nn.silu(second_pre).astype(jnp.bfloat16)
    head_out = jnp.dot(second_act, head_low, preferred_element_type=jnp.float32) + bias_head
    logits = head_out[:, :classes]
    deltas = head_out[:, classes:]
    largest = jnp.max(logits, axis=1, keepdims=True)
    shifted = jnp.exp(logits - largest)
    exp_total = jnp.sum(shifted, axis=1, keepdims=True)
    log_total = largest[:, 0] + jnp.log(exp_total[:, 0])
    label_hot = labels[:, None] == jnp.arange(classes, dtype=jnp.int32)[None, :]
    chosen = jnp.sum(jnp.where(label_hot, logits, 0.0), axis=1)
    foreground = (labels > 0).astype(jnp.float32)
    residue = deltas - targets.astype(jnp.float32) / FIXED_POINT
    region_loss = log_total - chosen + foreground * jnp.sum(huber_loss(residue), axis=1)
    decoded = decode_boxes(region_boxes, deltas)
    grad_logits = (shifted / exp_total - label_hot.astype(jnp.float32)) * loss_scale
    grad_deltas = foreground[:, None] * jnp.clip(residue, -1.0, 1.0) * loss_scale
    grad_out = jnp.concatenate([grad_logits, grad_deltas], axis=1).astype(jnp.bfloat16)
    head_term = cols_by_cols(second_act, grad_out)
    grad_second_act = rows_by_rows(grad_out, head_low)
    grad_second = (grad_second_act * silu_slope(second_pre)).astype(jnp.bfloat16)
    second_term = cols_by_cols(first_act, grad_second)
    second_gradient = lax.psum_scatter(second_term, ("dp", "roi"), scatter_dimension=0, tiled=True)
    grad_first_act = rows_by_rows(grad_second, second_full)
    grad_first = (grad_first_act * silu_slope(first_pre)).astype(jnp.bfloat16)
    group_count = lax.axis_size("dp")
    member_count = lax.axis_size("roi")
    owned_rows = first_weight.shape[0]
    split_columns = pooled_low.reshape(region_count, group_count, member_count, owned_rows)
    member_columns = lax.all_to_all(split_columns, "roi", split_axis=2, concat_axis=0, tiled=True)
    member_columns = member_columns.reshape(member_count * region_count, group_count * owned_rows)
    group_grads = lax.all_gather(grad_first, "roi", axis=0, tiled=True)
    member_term = cols_by_cols(member_columns, group_grads)
    first_gradient = lax.psum_scatter(member_term, "dp", scatter_dimension=0, tiled=True)
    grad_pooled = rows_by_rows(
        grad_first, lax.all_gather(first_low, ("dp", "roi"), axis=0, tiled=True)
    )
    grad_samples = grad_pooled.reshape(region_count, -1, channels)
    segment_total = image_count * cell_count
    map_partial = jax.ops.segment_sum(
        (corner_weights[:, :, 0:1] * grad_samples).reshape(-1, channels),
        flat_rows[:, :, 0].reshape(-1),
        num_segments=segment_total,
    )
    for corner in range(1, 4):
        map_partial = map_partial + jax.ops.segment_sum(
            (corner_weights[:, :, corner : corner + 1] * grad_samples).reshape(-1, channels),
            flat_rows[:, :, corner].reshape(-1),
            num_segments=segment_total,
        )
    map_partial = map_partial.reshape(image_count, cell_count, channels)
    map_gradient = lax.psum_scatter(map_partial, "roi", scatter_dimension=1, tiled=True)
    bias_term = jnp.concatenate(
        [
            jnp.sum(grad_first, axis=0, dtype=jnp.float32),
            jnp.sum(grad_second, axis=0, dtype=jnp.float32),
            jnp.sum(grad_out, axis=0, dtype=jnp.float32),
        ]
    )
    head_gradient, bias_gradient = lax.psum((head_term, bias_term), ("dp", "roi"))
    first_rounded = first_gradient.astype(jnp.bfloat16)
    second_rounded = second_gradient.astype(jnp.bfloat16)
    first_reduced, second_reduced = (
        lax.all_gather(first_rounded, ("dp", "roi"), axis=0, tiled=True),
        lax.all_gather(second_rounded, ("dp", "roi"), axis=0, tiled=True),
    )
    right_first_full, right_second_full = (
        lax.all_gather(right_first_root, ("dp", "roi"), axis=0, tiled=True),
        lax.all_gather(right_second_root, ("dp", "roi"), axis=0, tiled=True),
    )
    owner = lax.axis_index(("dp", "roi"))
    new_left_first, new_right_first, new_first_weight = shampoo_rows(
        first_rounded,
        first_reduced,
        first_weight,
        left_first,
        left_first_root,
        right_first,
        right_first_full,
        RATE_FIRST,
        owner * right_first.shape[0],
    )
    new_left_second, new_right_second, new_second_weight = shampoo_rows(
        second_rounded,
        second_reduced,
        second_weight,
        left_second,
        left_second_root,
        right_second,
        right_second_full,
        RATE_SECOND,
        owner * right_second.shape[0],
    )
    new_head_moment, new_head_weight = diagonal_step(
        head_gradient, head_weight, head_moment, RATE_HEAD
    )
    new_bias_moment, new_biases = diagonal_step(bias_gradient, biases, bias_moment, RATE_BIAS)
    return (
        region_loss,
        decoded,
        map_gradient,
        first_gradient,
        new_left_first,
        new_right_first,
        new_first_weight,
        second_gradient,
        new_left_second,
        new_right_second,
        new_second_weight,
        head_gradient,
        new_head_moment,
        new_head_weight,
        bias_gradient,
        new_bias_moment,
        new_biases,
    )


def solution(mesh):
    return jax.shard_map(
        local,
        mesh=mesh,
        in_specs=(
            P("dp", None, None),
            P(("dp", "roi"), None),
            P(("dp", "roi")),
            P(("dp", "roi")),
            P(("dp", "roi")),
            P(("dp", "roi"), None),
            P(("dp", "roi"), None),
            P(("dp", "roi"), None),
            P(),
            P(),
            P(),
            P(),
            P(("dp", "roi"), None),
            P(("dp", "roi"), None),
            P(("dp", "roi"), None),
            P(("dp", "roi"), None),
            P(("dp", "roi"), None),
            P(("dp", "roi"), None),
            P(("dp", "roi"), None),
            P(("dp", "roi"), None),
        ),
        out_specs=(
            P(("dp", "roi")),
            P(("dp", "roi"), None),
            P("dp", "roi", None),
            P(("dp", "roi"), None),
            P(("dp", "roi"), None),
            P(("dp", "roi"), None),
            P(("dp", "roi"), None),
            P(("dp", "roi"), None),
            P(("dp", "roi"), None),
            P(("dp", "roi"), None),
            P(("dp", "roi"), None),
            P(),
            P(),
            P(),
            P(),
            P(),
            P(),
        ),
        check_vma=False,
    )
```

profile of v0, /device:TPU:0, one launch (start us, length us, event | category | flops | bytes accessed | tf_op | source)
XLA Modules:
  0.0 1447.3 jit_solution(17253481171772571004)
XLA Ops:
  15.9 40.3 %gather_fusion.3 = bf16[14112,256]{1,0:T(8,128)(2,1)} fusion(bf16[5440,256]{1,0:T(8,128)(2,1)S(1)} %bitcast.62, s32[14336]{0:T(1024)S(1)} %pad_clamp_fusion), kind=kCustom, calls=%fused_computation.3 | custom fusion | bytes 14507136 | tf_op jit(solution)/shard_map/gather | solution.py:171
  68.2 40.3 %gather_fusion.2 = bf16[14112,256]{1,0:T(8,128)(2,1)} fusion(bf16[5440,256]{1,0:T(8,128)(2,1)S(1)} %bitcast.61, s32[14336]{0:T(1024)S(1)} %pad_clamp_fusion.1), kind=kCustom, calls=%fused_computation.2 | custom fusion | bytes 14507136 | tf_op jit(solution)/shard_map/gather | solution.py:171
  108.5 11.7 reshape.1014
  120.6 40.3 %gather_fusion.1 = bf16[14112,256]{1,0:T(8,128)(2,1)} fusion(bf16[5440,256]{1,0:T(8,128)(2,1)S(1)} %bitcast.60, s32[14336]{0:T(1024)S(1)} %pad_clamp_fusion.2), kind=kCustom, calls=%fused_computation.1 | custom fusion | bytes 14507136 | tf_op jit(solution)/shard_map/gather | solution.py:171
  160.8 11.9 reshape.1013
  173.1 40.3 %gather_fusion = bf16[14112,256]{1,0:T(8,128)(2,1)} fusion(bf16[5440,256]{1,0:T(8,128)(2,1)S(1)} %bitcast.59, s32[14336]{0:T(1024)S(1)} %pad_clamp_fusion.3), kind=kCustom, calls=%fused_computation | custom fusion | bytes 14507136 | tf_op jit(solution)/shard_map/gather | solution.py:168
  213.4 11.8 reshape.1012
  231.3 26.1 %add_convert_fusion = bf16[288,49,256]{2,1,0:T(8,128)(2,1)} fusion(f32[288,49,256]{2,1,0:T(8,128)} %reshape.1015, f32[288,49,256]{2,1,0:T(8,128)} %reshape.1014, f32[288,49,256]{2,1,0:T(8,128)} %reshape.1013, f32[288,49,256]{2,1,0:T(8,128)} %reshape.1012, f32[288,49]{1,0:T(8,128)S(1)} %reshape.1019, f32[288,49]{1,0:T(8,128)S(1)} %reshape.1018, ...), kind=kLoop, calls=%fused_computation.10 | loop fusion | flops 28901376 | bytes 65253888 | tf_op jit(solution)/shard_map/convert_element_type | solution.py:173
  266.6 15.5 %convolution_add_fusion.1 = f32[288,1024]{1,0:T(8,128)} fusion(bf16[288,12544]{1,0:T(8,128)(2,1)} %bitcast.66, bf16[12544,1024]{1,0:T(8,128)(2,1)} %all-gather.8.cloned.1.call-done, f32[1024]{0:T(1024)S(1)} %get-tuple-element.58), kind=kOutput, calls=%fused_computation.34 | convolution fusion | flops 7399047168 | bytes 34099200 | tf_op jit(solution)/shard_map/dot_general | solution.py:181
  294.3 24.8 %reshape.939 = bf16[288,16,2,392]{3,2,1,0:T(2,128)(2,1)} reshape(bf16[288,49,256]{2,1,0:T(8,128)(2,1)} %add_convert_fusion) | data formatting | bytes 14450688 | tf_op jit(solution)/shard_map/convert_element_type | solution.py:173
  328.6 190.2 %all_to_all.15 = bf16[288,16,2,392]{3,1,0,2:T(8,128)(2,1)} all-to-all(bf16[288,16,2,392]{3,1,0,2:T(8,128)(2,1)} %copy.122), channel_id=1, replica_groups=mesh['dp'=16,'roi'=2] {'roi'}, dimensions={2} | all-to-all | bytes 14450688 | tf_op jit(solution)/shard_map/all_to_all | solution.py:219
  518.7 16.6 %reshape.935 = bf16[576,6272]{1,0:T(8,128)(2,1)} reshape(bf16[2,288,16,1,392]{4,2,1,0,3:T(8,128)(2,1)} %bitcast.64) | data formatting | bytes 14450688 | tf_op jit(solution)/shard_map/reshape | solution.py:220
  535.4 18.3 %fusion.71 = f32[6272,1024]{1,0:T(8,128)} fusion(bf16[576,6272]{1,0:T(8,128)(2,1)} %reshape.935, bf16[576,1024]{1,0:T(8,128)(2,1)} %all-gather.12.cloned.1.call-done), kind=kOutput, calls=%fused_computation.147 | convolution fusion | flops 7398752256 | bytes 34095104 | tf_op jit(solution)/shard_map/dot_general | solution.py:104
  557.3 244.0 %reduce-scatter.6.cloned.1.call-done = f32[392,1024]{1,0:T(8,128)} async-done(((f32[6272,1024]{1,0:T(8,128)}), f32[392,1024]{1,0:T(8,128)}) %reduce-scatter.6.cloned.1.call-update) | async-done | bytes 1605648 | tf_op jit(solution)/shard_map/reduce_scatter | solution.py:223
  814.2 18.6 %fusion.70 = f32[288,12544]{1,0:T(8,128)} fusion(bf16[288,1024]{1,0:T(8,128)(2,1)S(1)} %copy-done.7, bf16[12544,1024]{1,0:T(8,128)(2,1)} %all-gather.8.cloned.1.call-done), kind=kOutput, calls=%fused_computation.146 | convolution fusion | flops 7398752256 | bytes 40730624 | tf_op jit(solution)/shard_map/dot_general | solution.py:98
  832.9 14.8 %reshape.933 = f32[14112,256]{1,0:T(8,128)} reshape(f32[288,12544]{1,0:T(8,128)} %fusion.70) | data formatting | bytes 28901376 | tf_op jit(solution)/shard_map/reshape | solution.py:227
  847.8 111.1 %scatter_custom_fusion = f32[5440,256]{1,0:T(8,128)} fusion(s32[14112]{0:T(1024)S(1)} %reshape.974, f32[14112,256]{1,0:T(8,128)} %reshape.933, f32[14112]{0:T(1024)S(1)} %copy-done.13, f32[]{:T(128)} %constant.34.clone.1), kind=kCustom, calls=%fused_computation.17 | custom fusion | flops 7225344 | bytes 20078596 | tf_op jit(solution)/shard_map/scatter-add | solution.py:229
  958.9 111.2 %scatter_custom_fusion.1 = f32[5440,256]{1,0:T(8,128)} fusion(s32[14112]{0:T(1024)S(1)} %reshape.982, f32[14112,256]{1,0:T(8,128)} %reshape.933, f32[14112]{0:T(1024)S(1)} %copy-done.12, f32[]{:T(128)} %constant.34.clone.1), kind=kCustom, calls=%fused_computation.15 | custom fusion | flops 7225344 | bytes 20078596 | tf_op jit(solution)/shard_map/scatter-add | solution.py:235
  1077.5 111.0 %scatter_custom_fusion.3 = f32[5440,256]{1,0:T(8,128)} fusion(s32[14112]{0:T(1024)S(1)} %reshape.998, f32[14112,256]{1,0:T(8,128)} %reshape.933, f32[14112]{0:T(1024)S(1)} %mul.573, f32[]{:T(128)} %constant.34.clone.1), kind=kCustom, calls=%fused_computation.11 | custom fusion | flops 7225344 | bytes 20078596 | tf_op jit(solution)/shard_map/scatter-add | solution.py:235
  1188.5 113.5 %scatter_custom_fusion.2 = f32[5440,256]{1,0:T(8,128)} fusion(f32[5440,256]{1,0:T(8,128)} %add.464, s32[14112]{0:T(1024)S(1)} %reshape.990, f32[14112,256]{1,0:T(8,128)} %reshape.933, f32[14112]{0:T(1024)S(1)} %copy-done.14), kind=kCustom, calls=%fused_computation.13 | custom fusion | flops 7225344 | bytes 20078592 | tf_op jit(solution)/shard_map/scatter-add | solution.py:235
  1309.6 40.0 %psum.15 = f32[2133]{0:T(1024)S(1)} all-reduce(f32[2133]{0:T(1024)S(1)} %pad_maximum_fusion.3), channel_id=1, replica_groups=mesh['dp'=16,'roi'=2] {'dp','roi'}, use_global_device_ids=true, to_apply=%region_17.18 | all-reduce | flops 2133 | bytes 17064 | tf_op jit(solution)/shard_map/psum | solution.py:249
  1367.0 20.9 %fusion.8 = f32[1024,392]{0,1:T(8,128)} fusion(bf16[12544,1024]{1,0:T(8,128)(2,1)} %all-gather.14.cloned.1.call-done, f32[392,12544]{1,0:T(8,128)} %param.35), kind=kOutput, calls=%fused_computation.19 | convolution fusion | flops 10075441152 | bytes 46964736 | tf_op jit(solution)/shard_map/dot_general | solution.py:123
  1397.0 15.8 %fusion.26 = f32[32,1024]{1,0:T(8,128)} fusion(bf16[12544,1024]{1,0:T(8,128)(2,1)} %all-gather.14.cloned.1.call-done, s32[]{:T(128)S(6)} %select_n.43, f32[32,1024]{1,0:T(8,128)S(1)} %copy-done.15), kind=kOutput, calls=%fused_computation.49 | convolution fusion | flops 822181888 | bytes 29163524 | tf_op jit(solution)/shard_map/dot_general | solution.py:104
  1412.7 26.8 %multiply_add_fusion = f32[392,12544]{1,0:T(8,128)} fusion(f32[392,12544]{1,0:T(8,128)} %param.34, bf16[392,1024]{1,0:T(8,128)(2,1)} %convert_element_type.169, bf16[12544,1024]{1,0:T(8,128)(2,1)} %all-gather.14.cloned.1.call-done), kind=kOutput, calls=%fused_computation.9 | convolution fusion | flops 10085275648 | bytes 65830912 | tf_op jit(solution)/shard_map/dot_general | solution.py:98
  (186 shorter events, 116.6 us)
Async XLA Ops:
  7.2 259.3 %all-gather.8.cloned.1.call-start = ((), (), s32[]{:S(2)}) async-start(), calls=%async_computation.4 | async-start | bytes 26492928 | tf_op jit(solution)/shard_map/all_gather | solution.py:183
  9.9 272.2 %all-gather.10.cloned.1.call-start = ((), (), s32[]{:S(2)}) async-start(), calls=%async_computation.5 | async-start | bytes 2162688 | tf_op jit(solution)/shard_map/all_gather | solution.py:188
  11.5 523.9 %all-gather.12.cloned.1.call-start = ((), (), s32[]{:S(2)}) async-start(), calls=%async_computation.7 | async-start | bytes 1769472 | tf_op jit(solution)/shard_map/all_gather | solution.py:221
  289.4 265.5 %reduce-scatter.8.cloned.1.call-start = ((), (), s32[]{:S(2)}) async-start(), calls=%async_computation.11 | async-start | bytes 4325376 | tf_op jit(solution)/shard_map/reduce_scatter | solution.py:212
  294.3 507.1 %reduce-scatter.6.cloned.1.call-start = ((), (), s32[]{:S(2)}) async-start(), calls=%async_computation.8 | async-start | bytes 27295744 | tf_op jit(solution)/shard_map/reduce_scatter | solution.py:223
  553.7 259.9 %copy-start.11 = (s32[288,49,1]{0,1,2:T(8,128)S(1)}, s32[288,49,1]{0,1,2:T(8,128)}, u32[]{:S(2)}) copy-start(s32[288,49,1]{0,1,2:T(8,128)} %get-tuple-element.44) | copy-start | bytes 169348
  553.7 260.2 %copy-start.10 = (s32[288,49,1]{0,1,2:T(8,128)S(1)}, s32[288,49,1]{0,1,2:T(8,128)}, u32[]{:S(2)}) copy-start(s32[288,49,1]{0,1,2:T(8,128)} %get-tuple-element.39) | copy-start | bytes 169348
  553.7 797.7 %all-reduce.2.cloned.1.call-start = ((), (), s32[]{:S(2)}) async-start(), calls=%async_computation.14 | async-start | bytes 720896 | tf_op jit(solution)/shard_map/psum | solution.py:249
  554.8 259.5 %copy-start.7 = (bf16[288,1024]{1,0:T(8,128)(2,1)S(1)}, bf16[288,1024]{1,0:T(8,128)(2,1)}, u32[]{:S(2)}) copy-start(bf16[288,1024]{1,0:T(8,128)(2,1)} %get-tuple-element.84) | copy-start | bytes 1769476
  554.8 798.7 %all-gather.18.cloned.1.call-start = ((), (), s32[]{:S(2)}) async-start(), calls=%async_computation.12 | async-start | bytes 2162688 | tf_op jit(solution)/shard_map/all_gather | solution.py:254
  556.5 805.1 %all-gather.20.cloned.1.call-start = ((), (), s32[]{:S(2)}) async-start(), calls=%async_computation.13 | async-start | bytes 4325376 | tf_op jit(solution)/shard_map/all_gather | solution.py:258
  557.2 809.7 %all-gather.14.cloned.1.call-start = ((), (), s32[]{:S(2)}) async-start(), calls=%async_computation.9 | async-start | bytes 26492928 | tf_op jit(solution)/shard_map/all_gather | solution.py:253
  803.8 584.1 %all-gather.16.cloned.1.call-start = ((), (), s32[]{:S(2)}) async-start(), calls=%async_computation.10 | async-start | bytes 4325376 | tf_op jit(solution)/shard_map/all_gather | solution.py:257
  804.4 635.2 %reduce-scatter.4.cloned.1.call-start = ((), (), s32[]{:S(2)}) async-start(), calls=%async_computation.6 | async-start | bytes 8355840 | tf_op jit(solution)/shard_map/reduce_scatter | solution.py:241
  847.8 111.1 %copy-start.12 = (f32[14112]{0:T(1024)S(1)}, f32[14112]{0:T(1024)}, u32[]{:S(2)}) copy-start(f32[14112]{0:T(1024)} %mul.567) | copy-start | bytes 169348
  1077.5 111.0 %copy-start.14 = (f32[14112]{0:T(1024)S(1)}, f32[14112]{0:T(1024)}, u32[]{:S(2)}) copy-start(f32[14112]{0:T(1024)} %mul.570) | copy-start | bytes 169348
  1309.4 40.2 %copy-start.21 = (f32[2133]{0:T(1024)S(1)}, f32[2133]{0:T(1024)}, u32[]{:S(2)}) copy-start(f32[2133]{0:T(1024)} %param.31) | copy-start | bytes 25600
  1309.4 40.3 %copy-start.24 = (f32[2133]{0:T(1024)S(1)}, f32[2133]{0:T(1024)}, u32[]{:S(2)}) copy-start(f32[2133]{0:T(1024)} %param.33) | copy-start | bytes 25600
  1309.4 40.9 %copy-start.30 = (pred[288]{0:T(512)(128)(4,1)S(1)}, pred[288]{0:T(512)(128)(4,1)}, u32[]{:S(2)}) copy-start(pred[288]{0:T(512)(128)(4,1)} %get-tuple-element.28) | copy-start | bytes 868
  1309.4 42.1 %copy-start.5 = (f32[1024,85]{0,1:T(8,128)S(1)}, f32[1024,85]{0,1:T(8,128)}, u32[]{:S(2)}) copy-start(f32[1024,85]{0,1:T(8,128)} %param.30) | copy-start | bytes 1044484
  1309.4 42.1 %copy-start.9 = (f32[1024,85]{0,1:T(8,128)S(1)}, f32[1024,85]{0,1:T(8,128)}, u32[]{:S(2)}) copy-start(f32[1024,85]{0,1:T(8,128)} %param.32) | copy-start | bytes 1044484
  1309.4 44.1 %copy-start.6 = (bf16[32,1024]{1,0:T(8,128)(2,1)S(1)}, bf16[32,1024]{1,0:T(8,128)(2,1)}, u32[]{:S(2)}) copy-start(bf16[32,1024]{1,0:T(8,128)(2,1)} %convert_element_type.171) | copy-start | bytes 196612
  1309.4 44.1 %copy-start.16 = (f32[32,1024]{1,0:T(8,128)S(1)}, f32[32,1024]{1,0:T(8,128)}, u32[]{:S(2)}) copy-start(f32[32,1024]{1,0:T(8,128)} %param.38) | copy-start | bytes 393220
  1309.4 47.1 %copy-start.17 = (f32[32,1024]{1,0:T(8,128)S(1)}, f32[32,1024]{1,0:T(8,128)}, u32[]{:S(2)}) copy-start(f32[32,1024]{1,0:T(8,128)} %param.39) | copy-start | bytes 393220
  (22 other events, 231.2 us)
Sparse Core Ops, SparseCore 0:
  11.5 159.8 all-gather.7
  174.9 54.7 all-gather.9
  289.5 25.4 all-gather.11
  317.7 175.5 reduce-scatter.7
  553.8 247.4 reduce-scatter.5
  807.1 125.5 all-reduce.1
  936.7 56.6 all-gather.17
  996.8 60.9 all-gather.19
  1061.0 155.6 all-gather.13
  1220.0 60.2 all-gather.15
  1349.7 69.1 reduce-scatter.3
where the time goes:
time: 1460 us; the launch traced here: 1450 us
  other arithmetic  506 us (35%)
  local copies, waits for them, and re-layouts  299 us (20%)
  waiting for transfers between devices  245 us (17%)
  blocking collectives  230 us (16%)
  matrix products  151 us (10%)
  between operations  15 us (1%)
    scatter-add x3, other arithmetic, local(): jax.ops.segment_sum((corner_weights[:, :, corner:corner + 1] * grad_sampl...  336 us
    reduce_scatter x1, waiting for transfers between devices, local(): lax.psum_scatter(member_term, 'dp', scatter_dimension=0, tiled=True)  244 us
    all_to_all x1, blocking collectives, local(): lax.all_to_all(split_columns, 'roi', split_axis=2, concat_axis=0, tiled=T...  190 us
    gather x3, local copies, waits for them, and re-layouts, local(): flat_maps[flat_rows[:, :, corner]]  121 us
    scatter-add x1, other arithmetic, local(): jax.ops.segment_sum((corner_weights[:, :, 0:1] * grad_samples).reshape(-1...  111 us
    dot_general x5, matrix products, rows_by_rows(): lax.dot_general(left_side, right_side, (((1,), (1,)), ((), ())), preferre...  52.1 us
    dot_general x5, matrix products, cols_by_cols(): lax.dot_general(left_side, right_side, (((0,), (0,)), ((), ())), preferre...  42.8 us
    gather x1, local copies, waits for them, and re-layouts, local(): pooled = corner_weights[:, :, 0:1] * flat_maps[flat_rows[:, :, 0]]  40.3 us
  transfers between devices with their start and end apart: 11, of which 1 were waited for; matrix products, arithmetic and copies ran while one was open for 65% of the time, Pallas kernels for 0%

commit v1 on v0

v1 whole, which is shorter than its diff:
```python
import functools

import jax
import jax.numpy as jnp
from jax import lax
from jax.experimental import pallas as pl
from jax.experimental.pallas import tpu as pltpu
from jax.sharding import PartitionSpec as P

POOL = 7
BINS = POOL * POOL
MAP = 32
TILE = 16
FINE = MAP * MAP
COLS = 896
MIB = 1 << 20

BETA = 0.95
DECAY = 0.99
RATE_FIRST = 0.01
RATE_SECOND = 0.03
RATE_HEAD = 0.005
RATE_BIAS = 0.05
EPSILON = 1e-08
FIXED_POINT = 4096.0


def round_up(value, unit):
    return (value + unit - 1) // unit * unit


def sample_points(boxes, levels):
    centers = (jnp.arange(POOL, dtype=jnp.float32) + 0.5) / POOL
    side = (MAP >> levels).astype(jnp.float32)[:, None]
    across = boxes[:, 0:1] + centers[None, :] * (boxes[:, 2:3] - boxes[:, 0:1])
    downward = boxes[:, 1:2] + centers[None, :] * (boxes[:, 3:4] - boxes[:, 1:2])
    across = jnp.clip(across * side - 0.5, 0.0, side - 1.0)
    downward = jnp.clip(downward * side - 0.5, 0.0, side - 1.0)
    return across, downward


def decode_boxes(region_boxes, deltas):
    widths = region_boxes[:, 2] - region_boxes[:, 0]
    heights = region_boxes[:, 3] - region_boxes[:, 1]
    center_x = region_boxes[:, 0] + 0.5 * widths
    center_y = region_boxes[:, 1] + 0.5 * heights
    moved_x = center_x + deltas[:, 0] / 10.0 * widths
    moved_y = center_y + deltas[:, 1] / 10.0 * heights
    new_width = widths * jnp.exp(deltas[:, 2] / 5.0)
    new_height = heights * jnp.exp(deltas[:, 3] / 5.0)
    return jnp.stack(
        [
            moved_x - 0.5 * new_width,
            moved_y - 0.5 * new_height,
            moved_x + 0.5 * new_width,
            moved_y + 0.5 * new_height,
        ],
        axis=1,
    )


def huber_loss(residue):
    magnitude = jnp.abs(residue)
    return jnp.where(magnitude < 1.0, 0.5 * residue * residue, magnitude - 0.5)


def silu_slope(values):
    sigmoid = jax.nn.sigmoid(values)
    return sigmoid * (1.0 + values * (1.0 - sigmoid))


def rows_by_rows(left_side, right_side):
    return lax.dot_general(
        left_side, right_side, (((1,), (1,)), ((), ())), preferred_element_type=jnp.float32
    )


def cols_by_cols(left_side, right_side):
    return lax.dot_general(
        left_side, right_side, (((0,), (0,)), ((), ())), preferred_element_type=jnp.float32
    )


def hat(distance):
    return jnp.maximum(1.0 - jnp.abs(distance), 0.0)


def in_order(from_shift):
    members = len(from_shift)
    me = lax.axis_index("roi")
    if members == 2:
        first = jnp.where(me == 0, from_shift[0], from_shift[1])
        second = jnp.where(me == 0, from_shift[1], from_shift[0])
        return jnp.stack([first, second])
    doubled = jnp.stack(from_shift + from_shift)
    return lax.dynamic_slice_in_dim(doubled, lax.rem(members - me, members), members, 0)


def gather_members(block):
    members = lax.axis_size("roi")
    got = [block]
    for shift in range(1, members):
        got.append(lax.ppermute(block, "roi", [((i + shift) % members, i) for i in range(members)]))
    return in_order(got)


def trade_members(parts):
    members = lax.axis_size("roi")
    me = lax.axis_index("roi")
    got = [lax.dynamic_index_in_dim(parts, me, 0, keepdims=False)]
    for shift in range(1, members):
        target = lax.rem(me + members - shift, members)
        part = lax.dynamic_index_in_dim(parts, target, 0, keepdims=False)
        got.append(lax.ppermute(part, "roi", [((i + shift) % members, i) for i in range(members)]))
    return in_order(got)


def lane_coordinates(rows, first_lane, lanes):
    cell = lax.broadcasted_iota(jnp.int32, (rows, lanes), 1) + first_lane
    return cell_coordinates(cell)


def cell_coordinates(cell):
    second = cell - FINE
    third = second - FINE // 4
    fourth = third - FINE // 16
    rest = cell - (FINE + FINE // 4 + FINE // 16 + FINE // 64)
    row = jnp.where(
        second < 0,
        cell >> 5,
        jnp.where(
            third < 0,
            second >> 4,
            jnp.where(fourth < 0, (third >> 3) + 32, (fourth >> 2) + 64),
        ),
    )
    column = jnp.where(
        second < 0,
        cell & 31,
        jnp.where(third < 0, second & 15, jnp.where(fourth < 0, third & 7, fourth & 3)),
    )
    row = jnp.where(rest < 0, row, 1000)
    return row.astype(jnp.float32), column.astype(jnp.float32)


def pool_kernel(fine_ref, coarse_ref, place_ref, maps_ref, out_ref, high, low, total):
    tile = pl.program_id(0)
    cells = maps_ref.shape[1]

    def part(first, count, column_of_row, start):
        chunk = 256 if count % 256 == 0 else 128
        for at in range(0, count, chunk):
            row_of, column_of = lane_coordinates(TILE, first + at, chunk)
            across = [hat(place_ref[:, j : j + 1] - column_of) for j in range(POOL)]
            for i in range(POOL):
                spot = column_of_row + i
                down = hat(place_ref[:, spot : spot + 1] - row_of)
                for j in range(POOL):
                    weight = down * across[j]
                    big = weight.astype(jnp.bfloat16)
                    rows = pl.ds((i * POOL + j) * TILE, TILE)
                    high[rows, pl.ds(at, chunk)] = big
                    low[rows, pl.ds(at, chunk)] = (weight - big.astype(jnp.float32)).astype(
                        jnp.bfloat16
                    )
        maps = maps_ref[0, pl.ds(first, count), :]
        product = jnp.dot(high[:, :count], maps, preferred_element_type=jnp.float32)
        product += jnp.dot(low[:, :count], maps, preferred_element_type=jnp.float32)
        if start:
            total[...] = product
        else:
            total[...] += product

    has_fine = fine_ref[tile] > 0
    has_coarse = coarse_ref[tile] > 0

    @pl.when(has_fine)
    def _():
        part(0, FINE, POOL, True)

    @pl.when(jnp.logical_not(has_fine))
    def _():
        total[...] = jnp.zeros_like(total)

    @pl.when(has_coarse)
    def _():
        part(FINE, cells - FINE, 2 * POOL, False)

    channels = maps_ref.shape[2]
    for b in range(BINS):
        out_ref[:, b * channels : (b + 1) * channels] = total[
            b * TILE : (b + 1) * TILE, :
        ].astype(jnp.bfloat16)


def pool(fine, coarse, places, maps, per_image):
    regions = places.shape[0]
    cells, channels = maps.shape[1:]
    tiles = per_image // TILE
    return pl.pallas_call(
        pool_kernel,
        grid_spec=pltpu.PrefetchScalarGridSpec(
            num_scalar_prefetch=2,
            grid=(regions // TILE,),
            in_specs=[
                pl.BlockSpec((TILE, 128), lambda t, *_: (t, 0)),
                pl.BlockSpec((1, cells, channels), lambda t, *_: (t // tiles, 0, 0)),
            ],
            out_specs=pl.BlockSpec((TILE, BINS * channels), lambda t, *_: (t, 0)),
            scratch_shapes=[
                pltpu.VMEM((BINS * TILE, FINE), jnp.bfloat16),
                pltpu.VMEM((BINS * TILE, FINE), jnp.bfloat16),
                pltpu.VMEM((BINS * TILE, channels), jnp.float32),
            ],
        ),
        out_shape=jax.ShapeDtypeStruct((regions, BINS * channels), jnp.bfloat16),
        compiler_params=pltpu.CompilerParams(vmem_limit_bytes=40 * MIB),
        cost_estimate=pl.CostEstimate(
            flops=4 * regions * BINS * 512 * channels,
            bytes_accessed=2 * regions * BINS * channels,
            transcendentals=0,
        ),
        name="pool",
    )(fine, coarse, places, maps)


def unpool_kernel(fine_ref, coarse_ref, place_ref, grad_ref, out_ref, weight, grads, *, tiles):
    tile = pl.program_id(0)
    cells, channels = out_ref.shape[1:]
    lanes = weight.shape[1]

    @pl.when(tile == 0)
    def _():
        grads[BINS * TILE :, :] = jnp.zeros_like(grads[BINS * TILE :, :])

    @pl.when(lax.rem(tile, tiles) == 0)
    def _():
        out_ref[...] = jnp.zeros_like(out_ref)

    for b in range(BINS):
        grads[b * TILE : (b + 1) * TILE, :] = grad_ref[:, b * channels : (b + 1) * channels]
    across = place_ref[0, 0:1, :]

    @pl.when(fine_ref[tile] > 0)
    def _():
        down = place_ref[0, 1:2, :]
        column = lax.broadcasted_iota(jnp.int32, (MAP, lanes), 0).astype(jnp.float32)
        over = hat(across - column)
        for y in range(MAP):
            weight[y * MAP : (y + 1) * MAP, :] = (hat(down - float(y)) * over).astype(jnp.bfloat16)
        out_ref[0, :FINE, :] += jnp.dot(
            weight[:FINE, :], grads[...], preferred_element_type=jnp.float32
        )

    @pl.when(coarse_ref[tile] > 0)
    def _():
        down = place_ref[0, 2:3, :]
        for at in range(FINE, cells, 16):
            cell = lax.broadcasted_iota(jnp.int32, (16, lanes), 0) + at
            row_of, column_of = cell_coordinates(cell)
            weight[at - FINE : at - FINE + 16, :] = (
                hat(down - row_of) * hat(across - column_of)
            ).astype(jnp.bfloat16)
        out_ref[0, FINE:, :] += jnp.dot(
            weight[: cells - FINE, :], grads[...], preferred_element_type=jnp.float32
        )


def unpool(fine, coarse, lane_places, grads, images, cells, channels):
    regions = grads.shape[0]
    count = regions // TILE
    tiles = count // images
    lanes = lane_places.shape[2]
    return pl.pallas_call(
        functools.partial(unpool_kernel, tiles=tiles),
        grid_spec=pltpu.PrefetchScalarGridSpec(
            num_scalar_prefetch=2,
            grid=(count,),
            in_specs=[
                pl.BlockSpec((1, 8, lanes), lambda t, *_: (t, 0, 0)),
                pl.BlockSpec((TILE, BINS * channels), lambda t, *_: (t, 0)),
            ],
            out_specs=pl.BlockSpec((1, cells, channels), lambda t, *_: (t // tiles, 0, 0)),
            scratch_shapes=[
                pltpu.VMEM((FINE, lanes), jnp.bfloat16),
                pltpu.VMEM((lanes, channels), jnp.bfloat16),
            ],
        ),
        out_shape=jax.ShapeDtypeStruct((images, cells, channels), jnp.float32),
        compiler_params=pltpu.CompilerParams(vmem_limit_bytes=40 * MIB),
        cost_estimate=pl.CostEstimate(
            flops=2 * regions * BINS * 512 * channels,
            bytes_accessed=2 * regions * BINS * channels,
            transcendentals=0,
        ),
        name="unpool",
    )(fine, coarse, lane_places, grads)


def shampoo_kernel(left_ref, root_ref, full_ref, own_ref, right_root_ref, weight_ref,
                   new_left_ref, new_weight_ref, mixed, *, rate):
    step = pl.program_id(0)
    members, _, width = full_ref.shape

    @pl.when(step == 0)
    def _():
        mixed[...] = jnp.zeros_like(mixed)

    root = root_ref[...].astype(jnp.bfloat16)
    gram = rows_by_rows(own_ref[0], full_ref[0])
    for member in range(1, members):
        gram += rows_by_rows(own_ref[member], full_ref[member])
    new_left_ref[...] = BETA * left_ref[...] + (1.0 - BETA) * gram
    for member in range(members):
        mixed[:, member * width : (member + 1) * width] += jnp.dot(
            root, full_ref[member], preferred_element_type=jnp.float32
        )

    @pl.when(step == pl.num_programs(0) - 1)
    def _():
        value = mixed[...]
        high = value.astype(jnp.bfloat16)
        low = (value - high.astype(jnp.float32)).astype(jnp.bfloat16)
        update = jnp.dot(high, right_root_ref[...], preferred_element_type=jnp.float32)
        update += jnp.dot(low, right_root_ref[...], preferred_element_type=jnp.float32)
        new_weight_ref[...] = weight_ref[...] - rate * update


def shampoo(left, root, full, own, right_root, weight, rate):
    rows, order = left.shape
    members, _, width = full.shape
    hidden = members * width
    return pl.pallas_call(
        functools.partial(shampoo_kernel, rate=rate),
        grid=(order // COLS,),
        in_specs=[
            pl.BlockSpec((rows, COLS), lambda t: (0, t)),
            pl.BlockSpec((rows, COLS), lambda t: (0, t)),
            pl.BlockSpec((members, COLS, width), lambda t: (0, t, 0)),
            pl.BlockSpec((members, rows, width), lambda t: (0, 0, 0)),
            pl.BlockSpec((hidden, hidden), lambda t: (0, 0)),
            pl.BlockSpec((rows, hidden), lambda t: (0, 0)),
        ],
        out_specs=[
            pl.BlockSpec((rows, COLS), lambda t: (0, t)),
            pl.BlockSpec((rows, hidden), lambda t: (0, 0)),
        ],
        out_shape=[
            jax.ShapeDtypeStruct((rows, order), jnp.float32),
            jax.ShapeDtypeStruct((rows, hidden), jnp.float32),
        ],
        scratch_shapes=[pltpu.VMEM((rows, hidden), jnp.float32)],
        compiler_params=pltpu.CompilerParams(vmem_limit_bytes=48 * MIB),
        cost_estimate=pl.CostEstimate(
            flops=4 * rows * order * hidden,
            bytes_accessed=12 * rows * order + 2 * order * hidden,
            transcendentals=0,
        ),
        name="shampoo",
    )(left, root, full, own, right_root, weight)


def diagonal_step(gradient, weight, moment, step_rate):
    new_moment = DECAY * moment + (1.0 - DECAY) * gradient * gradient
    return (new_moment, weight - step_rate * gradient / (jnp.sqrt(new_moment) + EPSILON))


def local(
    feature_maps,
    region_boxes,
    levels,
    labels,
    image_of_roi,
    targets,
    first_weight,
    second_weight,
    head_weight,
    biases,
    head_moment,
    bias_moment,
    left_first,
    left_first_root,
    right_first,
    right_first_root,
    left_second,
    left_second_root,
    right_second,
    right_second_root,
):
    groups = lax.axis_size("dp")
    members = lax.axis_size("roi")
    dp = lax.axis_index("dp")
    me = lax.axis_index("roi")
    owner = dp * members + me
    region_count = region_boxes.shape[0]
    group_regions = region_count * members
    images, cells, channels = feature_maps.shape
    per_image = group_regions // images
    owned, hidden = first_weight.shape
    width = hidden // members
    owned_second = second_weight.shape[0]
    features = owned * members * groups
    classes = head_weight.shape[1] - 4
    outs = classes + 4
    loss_scale = 1.0 / (region_count * groups * members)

    first_low = first_weight.astype(jnp.bfloat16)
    column_parts = jnp.swapaxes(first_low.reshape(owned, members, width), 0, 1)
    second_block = second_weight.astype(jnp.bfloat16).reshape(owned_second * members, width)
    parts = jnp.concatenate(
        [column_parts, jnp.broadcast_to(second_block, (members,) + second_block.shape)], axis=1
    )
    traded = trade_members(parts)
    payload = jnp.concatenate(
        [
            traded[:, :owned].reshape(members * owned, width),
            traded[:, owned:].reshape(members * members * owned_second, width),
        ],
        axis=0,
    )
    gathered = lax.all_gather(payload, "dp", axis=0)
    first_half = gathered[:, : members * owned].reshape(features, width)
    second_full = gathered[:, members * owned :].reshape(hidden, hidden)

    info = jnp.concatenate(
        [
            region_boxes,
            jnp.stack([levels, image_of_roi - dp * images, labels], axis=1).astype(jnp.float32),
            targets.astype(jnp.float32),
        ],
        axis=1,
    )
    info = gather_members(info).reshape(group_regions, info.shape[1])
    key = info[:, 5] * 4.0 + info[:, 4]
    number = jnp.arange(group_regions, dtype=jnp.int32)
    ahead = (key[None, :] < key[:, None]) | (
        (key[None, :] == key[:, None]) & (number[None, :] < number[:, None])
    )
    position = jnp.sum(ahead.astype(jnp.int32), axis=1)
    chosen = (position[None, :] == number[:, None]).astype(jnp.float32)
    info = jnp.dot(chosen, info, precision=lax.Precision.HIGHEST)
    boxes = info[:, :4]
    level = jnp.round(info[:, 4]).astype(jnp.int32)
    across, down = sample_points(boxes, level)
    fine_down = jnp.where(level[:, None] == 0, down, -64.0)
    coarse_down = jnp.where(
        level[:, None] == 0, -64.0, down + 32.0 * (level[:, None] - 1).astype(jnp.float32)
    )
    count = group_regions // TILE
    fine = jnp.max((level == 0).astype(jnp.int32).reshape(count, TILE), axis=1)
    coarse = jnp.max((level > 0).astype(jnp.int32).reshape(count, TILE), axis=1)
    places = jnp.pad(
        jnp.concatenate([across, fine_down, coarse_down], axis=1), ((0, 0), (0, 128 - 3 * POOL))
    )
    by_tile = places[:, : 3 * POOL].reshape(count, TILE, 3, POOL)
    by_tile = jnp.transpose(by_tile, (0, 2, 3, 1))
    lane_shape = (count, POOL, POOL, TILE)
    lanes = round_up(BINS * TILE, 128)
    lane_places = jnp.stack(
        [
            jnp.broadcast_to(by_tile[:, 0, None, :, :], lane_shape),
            jnp.broadcast_to(by_tile[:, 1, :, None, :], lane_shape),
            jnp.broadcast_to(by_tile[:, 2, :, None, :], lane_shape),
        ],
        axis=1,
    ).reshape(count, 3, BINS * TILE)
    lane_places = jnp.pad(lane_places, ((0, 0), (0, 5), (0, lanes - BINS * TILE)))

    padded_maps = jnp.pad(feature_maps, ((0, 0), (0, round_up(cells, 128) - cells), (0, 0)))
    pooled = pool(fine, coarse, places, padded_maps, per_image)

    head_low = head_weight.astype(jnp.bfloat16)
    bias_first = lax.dynamic_slice_in_dim(biases, me * width, width)
    bias_second = biases[hidden : 2 * hidden]
    bias_head = biases[2 * hidden :]
    first_pre = jnp.dot(pooled, first_half, preferred_element_type=jnp.float32) + bias_first
    first_act = jax.nn.silu(first_pre).astype(jnp.bfloat16)
    act_rows = trade_members(first_act.reshape(members, region_count, width))
    act_rows = jnp.swapaxes(act_rows, 0, 1).reshape(region_count, hidden)
    second_pre = jnp.dot(act_rows, second_full, preferred_element_type=jnp.float32) + bias_second
    second_act = jax.nn.silu(second_pre).astype(jnp.bfloat16)
    head_out = jnp.dot(second_act, head_low, preferred_element_type=jnp.float32) + bias_head
    own_info = lax.dynamic_slice_in_dim(info, me * region_count, region_count, 0)
    own_labels = jnp.round(own_info[:, 6]).astype(jnp.int32)
    logits = head_out[:, :classes]
    deltas = head_out[:, classes:]
    largest = jnp.max(logits, axis=1, keepdims=True)
    shifted = jnp.exp(logits - largest)
    exp_total = jnp.sum(shifted, axis=1, keepdims=True)
    log_total = largest[:, 0] + jnp.log(exp_total[:, 0])
    label_hot = own_labels[:, None] == jnp.arange(classes, dtype=jnp.int32)[None, :]
    picked = jnp.sum(jnp.where(label_hot, logits, 0.0), axis=1)
    foreground = (own_labels > 0).astype(jnp.float32)
    residue = deltas - own_info[:, 7:11] / FIXED_POINT
    loss = log_total - picked + foreground * jnp.sum(huber_loss(residue), axis=1)
    decoded = decode_boxes(own_info[:, :4], deltas)
    results = gather_members(jnp.concatenate([loss[:, None], decoded], axis=1))
    results = results.reshape(group_regions, 5)
    own_position = lax.dynamic_slice_in_dim(position, me * region_count, region_count)
    own_chosen = (own_position[:, None] == number[None, :]).astype(jnp.float32)
    results = jnp.dot(own_chosen, results, precision=lax.Precision.HIGHEST)

    grad_logits = (shifted / exp_total - label_hot.astype(jnp.float32)) * loss_scale
    grad_deltas = foreground[:, None] * jnp.clip(residue, -1.0, 1.0) * loss_scale
    grad_out = jnp.concatenate([grad_logits, grad_deltas], axis=1).astype(jnp.bfloat16)
    head_term = cols_by_cols(second_act, grad_out)
    grad_second_act = rows_by_rows(grad_out, head_low)
    grad_second = (grad_second_act * silu_slope(second_pre)).astype(jnp.bfloat16)
    group_second = gather_members(grad_second).reshape(group_regions, hidden)
    second_rows = lax.dynamic_slice_in_dim(second_full, me * width, width, 0)
    grad_first = (rows_by_rows(group_second, second_rows) * silu_slope(first_pre)).astype(
        jnp.bfloat16
    )
    first_term = cols_by_cols(pooled, grad_first)
    second_term = cols_by_cols(first_act, group_second)
    first_sum = lax.psum_scatter(first_term, "dp", scatter_dimension=0, tiled=True)
    second_sum = lax.psum_scatter(second_term, "dp", scatter_dimension=0, tiled=True)

    grad_pooled = rows_by_rows(grad_first, first_half).astype(jnp.bfloat16)
    map_partial = unpool(fine, coarse, lane_places, grad_pooled, images, cells, channels)
    map_parts = map_partial.reshape(images, members, cells // members, channels)
    map_parts = jnp.swapaxes(map_parts, 0, 1)
    map_own = lax.dynamic_index_in_dim(map_parts, me, 0, keepdims=False)
    map_traded = trade_members(map_parts.astype(jnp.bfloat16)).astype(jnp.float32)
    keep = (jnp.arange(members) == me)[:, None, None, None]
    map_gradient = map_own + jnp.sum(jnp.where(keep, 0.0, map_traded), axis=0)

    zeros = jnp.zeros((hidden,), jnp.float32)
    bias_term = jnp.concatenate(
        [
            lax.dynamic_update_slice_in_dim(
                zeros, jnp.sum(grad_first, axis=0, dtype=jnp.float32), me * width, 0
            ),
            jnp.sum(grad_second, axis=0, dtype=jnp.float32),
            jnp.sum(grad_out, axis=0, dtype=jnp.float32),
        ]
    )
    head_gradient, bias_gradient = lax.psum((head_term, bias_term), ("dp", "roi"))

    first_gradient = trade_members(first_sum.reshape(members, owned, width))
    first_gradient = jnp.swapaxes(first_gradient, 0, 1).reshape(owned, hidden)
    devices = groups * members
    second_gradient = lax.ppermute(
        second_sum,
        ("dp", "roi"),
        [((b % groups) * members + b // groups, b) for b in range(devices)],
    )
    first_reduced = lax.all_gather(first_sum.astype(jnp.bfloat16), ("roi", "dp"), axis=0)
    first_reduced = first_reduced.reshape(members, features, width)
    second_reduced = lax.all_gather(
        second_sum.astype(jnp.bfloat16), ("roi", "dp"), axis=0, tiled=True
    )
    right_roots = jnp.stack([right_first_root, right_second_root]).astype(jnp.bfloat16)
    right_roots = lax.all_gather(right_roots, ("dp", "roi"), axis=1, tiled=True)

    own_first = lax.dynamic_slice_in_dim(first_reduced, owner * owned, owned, 1)
    new_left_first, new_first_weight = shampoo(
        left_first, left_first_root, first_reduced, own_first, right_roots[0], first_weight,
        RATE_FIRST,
    )
    own_rows = right_first.shape[0]
    which = owner * own_rows // width
    own_columns = lax.dynamic_slice(
        first_reduced, (which, 0, owner * own_rows - which * width), (1, features, own_rows)
    )[0]
    first_gram = jnp.concatenate(
        [cols_by_cols(own_columns, first_reduced[member]) for member in range(members)], axis=1
    )
    new_right_first = BETA * right_first + (1.0 - BETA) * first_gram

    own_second = lax.dynamic_slice_in_dim(second_reduced, owner * owned_second, owned_second, 0)
    own_columns = lax.dynamic_slice_in_dim(second_reduced, owner * own_rows, own_rows, 1)
    new_left_second = BETA * left_second + (1.0 - BETA) * rows_by_rows(own_second, second_reduced)
    new_right_second = BETA * right_second + (1.0 - BETA) * cols_by_cols(
        own_columns, second_reduced
    )
    mixed = jnp.dot(
        left_second_root.astype(jnp.bfloat16), second_reduced, preferred_element_type=jnp.float32
    )
    mixed_high = mixed.astype(jnp.bfloat16)
    mixed_low = (mixed - mixed_high.astype(jnp.float32)).astype(jnp.bfloat16)
    update = jnp.dot(mixed_high, right_roots[1], preferred_element_type=jnp.float32) + jnp.dot(
        mixed_low, right_roots[1], preferred_element_type=jnp.float32
    )
    new_second_weight = second_weight - RATE_SECOND * update

    new_head_moment, new_head_weight = diagonal_step(
        head_gradient, head_weight, head_moment, RATE_HEAD
    )
    new_bias_moment, new_biases = diagonal_step(bias_gradient, biases, bias_moment, RATE_BIAS)
    return (
        results[:, 0],
        results[:, 1:],
        map_gradient,
        first_gradient,
        new_left_first,
        new_right_first,
        new_first_weight,
        second_gradient,
        new_left_second,
        new_right_second,
        new_second_weight,
        head_gradient,
        new_head_moment,
        new_head_weight,
        bias_gradient,
        new_bias_moment,
        new_biases,
    )


def solution(mesh):
    rows = P(("dp", "roi"), None)
    flat = P(("dp", "roi"))
    return jax.shard_map(
        local,
        mesh=mesh,
        in_specs=(P("dp", None, None), rows, flat, flat, flat, rows, rows, rows)
        + (P(),) * 4
        + (rows,) * 8,
        out_specs=(flat, rows, P("dp", "roi", None)) + (rows,) * 8 + (P(),) * 6,
        check_vma=False,
    )
```

time: 1460 us -> 869 us (0.60)
  other arithmetic: 506 us -> 27.4 us
  local copies, waits for them, and re-layouts: 299 us -> 34.3 us
  waiting for transfers between devices: 245 us -> 489 us
  blocking collectives: 230 us -> 64.4 us
  Pallas kernels: 0 us -> 120 us
  matrix products: 151 us -> 90.5 us
  starting transfers between devices: 0.45 us -> 21.7 us
    scatter-add x4 -> x0, other arithmetic: 447 us -> none  [the longest x3 336 us: local(): jax.ops.segment_sum((corner_weights[:, :, corner:corner + 1] * grad_sampl...]
    all_to_all x1 -> x0, blocking collectives: 190 us -> none  [local(): lax.all_to_all(split_columns, 'roi', split_axis=2, concat_axis=0, tiled=T...]
    gather x4 -> x0, local copies, waits for them, and re-layouts: 161 us -> none  [the longest x3 121 us: local(): flat_maps[flat_rows[:, :, corner]]]
    all_gather x7 -> x4, waiting for transfers between devices: 0.03 us -> 154 us  [the longest x1 89.4 us: local(): lax.all_gather(first_sum.astype(jnp.bfloat16), ('roi', 'dp'), axis=0)]
    pallas_call x0 -> x3, Pallas kernels: none -> 120 us  [the longest x1 45.4 us: pool(): pl.pallas_call(pool_kernel, grid_spec=pltpu.PrefetchScalarGridSpec(num_sc...]
    convert_element_type x6 -> x2, local copies, waits for them, and re-layouts: 81.4 us -> 0.14 us  [the longest x1 0.07 us: local(): coarse = jnp.max((level > 0).astype(jnp.int32).reshape(count, TILE), axis=1)]
    ppermute x0 -> x8, waiting for transfers between devices: none -> 50.8 us  [the longest x4 37.5 us: trade_members(): lax.ppermute(part, 'roi', [((i + shift) % members, i) for i in range(memb...]
    reduce_scatter x3 -> x2, waiting for transfers between devices: 244 us -> 284 us  [the longest x1 252 us: local(): lax.psum_scatter(first_term, 'dp', scatter_dimension=0, tiled=True)]
  transfers between devices with their start and end apart: 11 -> 15, of which waited for: 1 -> 8; matrix products, arithmetic and copies ran while one was open for 65% -> 10% of each run, Pallas kernels for 0% -> 9%
where the time goes in v1:
time: 869 us; the launch traced here: 864 us
  waiting for transfers between devices  489 us (56%)
  Pallas kernels  120 us (14%)
  matrix products  90.5 us (10%)
  blocking collectives  64.4 us (7%)
  local copies, waits for them, and re-layouts  34.3 us (4%)
  other arithmetic  27.4 us (3%)
  starting transfers between devices  21.7 us (2%)
  between operations  16.6 us (2%)
    reduce_scatter x1, waiting for transfers between devices, local(): lax.psum_scatter(first_term, 'dp', scatter_dimension=0, tiled=True)  252 us
    all_gather x1, waiting for transfers between devices, local(): lax.all_gather(first_sum.astype(jnp.bfloat16), ('roi', 'dp'), axis=0)  89.4 us
    all_gather x1, waiting for transfers between devices, local(): gathered = lax.all_gather(payload, 'dp', axis=0)  65 us
    psum x1, blocking collectives, local(): lax.psum((head_term, bias_term), ('dp', 'roi'))  64.4 us
    pallas_call x1, Pallas kernels, pool(): pl.pallas_call(pool_kernel, grid_spec=pltpu.PrefetchScalarGridSpec(num_sc...  45.4 us
    dot_general x6, matrix products, cols_by_cols(): lax.dot_general(left_side, right_side, (((0,), (0,)), ((), ())), preferre...  41 us
    pallas_call x1, Pallas kernels, shampoo(): pl.pallas_call(functools.partial(shampoo_kernel, rate=rate), grid=(order...  39.5 us
    ppermute x4, waiting for transfers between devices, trade_members(): lax.ppermute(part, 'roi', [((i + shift) % members, i) for i in range(memb...  37.5 us
  transfers between devices with their start and end apart: 15, of which 8 were waited for; matrix products, arithmetic and copies ran while one was open for 10% of the time, Pallas kernels for 9%

profile of v1, /device:TPU:0, one launch (start us, length us, event | category | flops | bytes accessed | tf_op | source)
XLA Modules:
  0.0 863.8 jit_solution(15341013347358791254)
XLA Ops:
  11.2 2.9 fusion.24
  14.2 3.0 collective-permute-start.1
  17.2 10.7 %collective-permute-done.1 = bf16[456,512]{1,0:T(8,128)(2,1)S(1)} collective-permute-done((bf16[456,512]{1,0:T(8,128)(2,1)S(1)}, bf16[456,512]{1,0:T(8,128)(2,1)S(1)}, u32[]{:S(2)}, u32[]{:S(2)}) %collective-permute-start.1) | collective-permute-done | bytes 466976 | tf_op jit(solution)/shard_map/ppermute | solution.py:114
  35.8 45.4 %pool.1 = bf16[576,12544]{1,0:T(8,128)(2,1)} custom-call(s32[36]{0:T(128)S(1)} %reduce_max.27.fine_ref, s32[36]{0:T(128)S(1)} %reduce_max.28.coarse_ref, f32[576,128]{1,0:T(8,128)S(1)} %pad.12.place_ref, bf16[4,1408,256]{2,1,0:T(8,128)(2,1)S(1)} %pad.13.maps_ref), custom_call_target="tpu_custom_call" | custom-call | flops 14797504512 | bytes 14450688 | tf_op jit(solution)/shard_map/pool/pallas_call | solution.py:200
  81.3 65.0 %all-gather.11.cloned.1.call-done = bf16[14592,512]{1,0:T(8,128)(2,1)} async-done(((bf16[912,512]{1,0:T(8,128)(2,1)}), bf16[14592,512]{1,0:T(8,128)(2,1)}) %all-gather.11.cloned.1.call-update) | async-done | bytes 14942224 | tf_op jit(solution)/shard_map/all_gather | solution.py:421
  146.3 6.4 slice.172
  152.7 16.4 %multiply_convert_fusion.1 = (bf16[576,512]{1,0:T(8,128)(2,1)S(1)}, f32[576,512]{1,0:T(8,128)}) fusion(f32[512]{0:T(512)S(1)} %dynamic_slice.53, bf16[576,12544]{1,0:T(8,128)(2,1)} %pool.1, bf16[12544,512]{1,0:T(8,128)(2,1)S(1)} %bitcast.145), kind=kOutput, calls=%fused_computation.39 | convolution fusion | flops 7400521728 | bytes 29067264 | tf_op jit(solution)/shard_map/dot_general | solution.py:476
  175.4 4.0 collective-permute-done.2
  186.0 13.2 %collective-permute-done.4 = bf16[288,1024]{1,0:T(8,128)(2,1)S(1)} collective-permute-done((bf16[288,1024]{1,0:T(8,128)(2,1)S(1)}, bf16[288,1024]{1,0:T(8,128)(2,1)S(1)}, u32[]{:S(2)}, u32[]{:S(2)}) %collective-permute-start.4) | collective-permute-done | bytes 589856 | tf_op jit(solution)/shard_map/ppermute | solution.py:103
  200.5 2.4 fusion.86
  204.4 3.3 convert_reduce_fusion.2
  208.5 20.7 %fusion.85 = f32[12544,512]{1,0:T(8,128)} fusion(bf16[576,12544]{1,0:T(8,128)(2,1)} %pool.1, bf16[576,512]{1,0:T(8,128)(2,1)S(1)} %get-tuple-element.77), kind=kOutput, calls=%fused_computation.190 | convolution fusion | flops 7398752256 | bytes 40730624 | tf_op jit(solution)/shard_map/dot_general | solution.py:79
  232.1 31.9 %reduce-scatter.5.cloned.1.call-done = f32[32,1024]{1,0:T(8,128)} async-done(((f32[512,1024]{1,0:T(8,128)}), f32[32,1024]{1,0:T(8,128)}) %reduce-scatter.5.cloned.1.call-update) | async-done | bytes 131088 | tf_op jit(solution)/shard_map/reduce_scatter | solution.py:517
  265.8 251.9 %reduce-scatter.3.cloned.1.call-done = f32[784,512]{1,0:T(8,128)} async-done(((f32[12544,512]{1,0:T(8,128)}), f32[784,512]{1,0:T(8,128)}) %reduce-scatter.3.cloned.1.call-update) | async-done | bytes 1605648 | tf_op jit(solution)/shard_map/reduce_scatter | solution.py:516
  517.7 2.4 convert_element_type.160
  525.2 19.8 %convolution_convert_fusion.grad_ref = bf16[576,12544]{1,0:T(8,128)(2,1)} fusion(bf16[576,512]{1,0:T(8,128)(2,1)S(1)} %copy-done.39, bf16[12544,512]{1,0:T(8,128)(2,1)} %bitcast.146), kind=kOutput, calls=%fused_computation | convolution fusion | flops 7405977600 | bytes 27885568 | tf_op jit(solution)/shard_map/dot_general | solution.py:73
  544.9 34.9 %unpool.1 = f32[4,1360,256]{2,1,0:T(8,128)S(1)} custom-call(s32[36]{0:T(128)S(1)} %reduce_max.27.fine_ref, s32[36]{0:T(128)S(1)} %reduce_max.28.coarse_ref, f32[36,8,896]{2,1,0:T(8,128)S(1)} %pad.14.place_ref, bf16[576,12544]{1,0:T(8,128)(2,1)} %convolution_convert_fusion.grad_ref), custom_call_target="tpu_custom_call" | custom-call | flops 7398752256 | bytes 14450688 | tf_op jit(solution)/shard_map/unpool/pallas_call | solution.py:274
  591.2 64.4 %psum.15 = f32[2133]{0:T(1024)S(1)} all-reduce(f32[2133]{0:T(1024)S(1)} %pad_maximum_fusion.13), channel_id=1, replica_groups=mesh['dp'=16,'roi'=2] {'dp','roi'}, use_global_device_ids=true, to_apply=%region_14.15 | all-reduce | flops 2133 | bytes 17064 | tf_op jit(solution)/shard_map/psum | solution.py:538
  667.3 9.0 %collective-permute-start.6 = (f32[392,512]{1,0:T(8,128)S(1)}, f32[392,512]{1,0:T(8,128)S(1)}, u32[]{:S(2)}, u32[]{:S(2)}) collective-permute-start(f32[392,512]{1,0:T(8,128)S(1)} %dynamic-slice_bitcast_fusion.1), channel_id=1, source_target_pairs={{1,0},{0,1},{3,2},{2,3},{5,4},{4,5},{7,6},{6,7},{9,8},{8,9},{11,10... | collective-permute-start | bytes 2408456 | tf_op jit(solution)/shard_map/ppermute | solution.py:114
  680.1 22.8 %collective-permute-done.6 = f32[392,512]{1,0:T(8,128)S(1)} collective-permute-done((f32[392,512]{1,0:T(8,128)S(1)}, f32[392,512]{1,0:T(8,128)S(1)}, u32[]{:S(2)}, u32[]{:S(2)}) %collective-permute-start.6) | collective-permute-done | bytes 802848 | tf_op jit(solution)/shard_map/ppermute | solution.py:114
  707.4 89.4 %all-gather.13.cloned.1.call-done = bf16[25088,512]{1,0:T(8,128)(2,1)} async-done(((bf16[784,512]{1,0:T(8,128)(2,1)}), bf16[25088,512]{1,0:T(8,128)(2,1)}) %all-gather.13.cloned.1.call-update) | async-done | bytes 25690128 | tf_op jit(solution)/shard_map/all_gather | solution.py:548
  798.0 7.9 fusion
  805.9 7.8 fusion.2
  814.4 39.5 %shampoo.1 = (f32[392,12544]{1,0:T(8,128)}, f32[392,1024]{1,0:T(8,128)}) custom-call(f32[392,12544]{1,0:T(8,128)} %left_ref.1, f32[392,12544]{1,0:T(8,128)} %root_ref.1, bf16[2,12544,512]{2,1,0:T(8,128)(2,1)} %bitcast.142, bf16[2,392,512]{2,1,0:T(8,128)(2,1)S(1)} %constant_dynamic-slice_fusion.1.own_ref, ...), custom_call_target="tpu_custom_call" | custom-call | flops 20141047808 | bytes 84697088 | tf_op jit(solution)/shard_map/shampoo/pallas_call | solution.py:333
  (227 shorter events, 72.2 us)
Async XLA Ops:
  8.0 138.3 %all-gather.11.cloned.1.call-start = ((), (), s32[]{:S(2)}) async-start(), calls=%async_computation.7 | async-start | bytes 15876096 | tf_op jit(solution)/shard_map/all_gather | solution.py:421
  14.2 13.7 %collective-permute-start.1 = (bf16[456,512]{1,0:T(8,128)(2,1)S(1)}, bf16[456,512]{1,0:T(8,128)(2,1)S(1)}, u32[]{:S(2)}, u32[]{:S(2)}) collective-permute-start(bf16[456,512]{1,0:T(8,128)(2,1)S(1)} %bitcast.161), channel_id=1, source_target_pairs={{1,0},{0,1},{3,2},{2,3},{5,4},{4,5},{7,6},{6,7},{9,8},{8,9},{11,10... | collective-permute-start | bytes 1400840 | tf_op jit(solution)/shard_map/ppermute | solution.py:114
  29.2 234.8 %reduce-scatter.5.cloned.1.call-start = ((), (), s32[]{:S(2)}) async-start(), calls=%async_computation.4 | async-start | bytes 2228224 | tf_op jit(solution)/shard_map/reduce_scatter | solution.py:517
  29.7 3.9 collective-permute-start
  35.0 136.3 %copy-start.24 = (f32[576,11]{0,1:T(8,128)}, f32[576,11]{0,1:T(8,128)S(1)}, u32[]{:S(2)}) copy-start(f32[576,11]{0,1:T(8,128)S(1)} %fusion.12) | copy-start | bytes 76036
  35.6 45.7 %copy-start.14 = (f32[576,21]{0,1:T(8,128)}, f32[576,21]{0,1:T(8,128)S(1)}, u32[]{:S(2)}) copy-start(f32[576,21]{0,1:T(8,128)S(1)} %pad_maximum_fusion.7) | copy-start | bytes 145156
  152.7 16.4 %copy-start.3 = (bf16[16,784,512]{2,1,0:T(8,128)(2,1)}, bf16[16,784,512]{2,1,0:T(8,128)(2,1)S(1)}, u32[]{:S(2)}) copy-start(bf16[16,784,512]{2,1,0:T(8,128)(2,1)S(1)} %slice.172) | copy-start | bytes 38535172
  169.9 9.5 %collective-permute-start.2 = (bf16[288,512]{1,0:T(8,128)(2,1)}, bf16[288,512]{1,0:T(8,128)(2,1)}, u32[]{:S(2)}, u32[]{:S(2)}) collective-permute-start(bf16[288,512]{1,0:T(8,128)(2,1)} %dynamic-slice_bitcast_fusion.2), channel_id=1, source_target_pairs={{1,0},{0,1},{3,2},{2,3},{5,4},{4,5},{7,6},{6,7},{9,8},{8,9},{11,10... | collective-permute-start | bytes 884744 | tf_op jit(solution)/shard_map/ppermute | solution.py:114
  184.5 14.7 %collective-permute-start.4 = (bf16[288,1024]{1,0:T(8,128)(2,1)S(1)}, bf16[288,1024]{1,0:T(8,128)(2,1)S(1)}, u32[]{:S(2)}, u32[]{:S(2)}) collective-permute-start(bf16[288,1024]{1,0:T(8,128)(2,1)S(1)} %get-tuple-element.75), channel_id=1, source_target_pairs={{1,0},{0,1},{3,2},{2,3},{5,4},{4,5},{7,6},{6,7},{9,8},{8,9},{11,10... | collective-permute-start | bytes 1769480 | tf_op jit(solution)/shard_map/ppermute | solution.py:103
  202.9 314.8 %reduce-scatter.3.cloned.1.call-start = ((), (), s32[]{:S(2)}) async-start(), calls=%async_computation.2 | async-start | bytes 27295744 | tf_op jit(solution)/shard_map/reduce_scatter | solution.py:516
  229.3 355.6 %all-gather.7.cloned.1.call-start = ((), (), s32[]{:S(2)}) async-start(), calls=%async_computation.3 | async-start | bytes 4325376 | tf_op jit(solution)/shard_map/all_gather | solution.py:554
  230.9 357.7 %all-reduce.5.cloned.1.call-start = ((), (), s32[]{:S(2)}) async-start(), calls=%async_computation.6 | async-start | bytes 720896 | tf_op jit(solution)/shard_map/psum | solution.py:538
  232.0 288.7 %copy-start.30 = (s32[576]{0:T(1024)S(1)}, s32[576]{0:T(1024)}, u32[]{:S(2)}) copy-start(s32[576]{0:T(1024)} %copy-done.29) | copy-start | bytes 6916
  232.0 289.3 %copy-start.15 = (f32[576,21]{0,1:T(8,128)S(1)}, f32[576,21]{0,1:T(8,128)}, u32[]{:S(2)}) copy-start(f32[576,21]{0,1:T(8,128)} %copy-done.14) | copy-start | bytes 145156
  232.0 430.7 %all-gather.9.cloned.1.call-start = ((), (), s32[]{:S(2)}) async-start(), calls=%async_computation.5 | async-start | bytes 2162688 | tf_op jit(solution)/shard_map/all_gather | solution.py:550
  265.5 531.3 %all-gather.13.cloned.1.call-start = ((), (), s32[]{:S(2)}) async-start(), calls=%async_computation.8 | async-start | bytes 26492928 | tf_op jit(solution)/shard_map/all_gather | solution.py:548
  523.7 63.1 %collective-permute-start.3 = (f32[288,5]{0,1:T(8,128)S(1)}, f32[288,5]{0,1:T(8,128)S(1)}, u32[]{:S(2)}, u32[]{:S(2)}) collective-permute-start(f32[288,5]{0,1:T(8,128)S(1)} %concatenate.29), channel_id=1, source_target_pairs={{1,0},{0,1},{3,2},{2,3},{5,4},{4,5},{7,6},{6,7},{9,8},{8,9},{11,10... | collective-permute-start | bytes 17288 | tf_op jit(solution)/shard_map/ppermute | solution.py:103
  584.3 71.9 %collective-permute-start.5 = (bf16[4,680,256]{2,1,0:T(8,128)(2,1)}, bf16[4,680,256]{2,1,0:T(8,128)(2,1)}, u32[]{:S(2)}, u32[]{:S(2)}) collective-permute-start(bf16[4,680,256]{2,1,0:T(8,128)(2,1)} %dynamic-slice_bitcast_fusion), channel_id=1, source_target_pairs={{1,0},{0,1},{3,2},{2,3},{5,4},{4,5},{7,6},{6,7},{9,8},{8,9},{11,10... | collective-permute-start | bytes 4177928 | tf_op jit(solution)/shard_map/ppermute | solution.py:114
  586.8 68.8 %copy-start.26 = (f32[2133]{0:T(1024)S(1)}, f32[2133]{0:T(1024)}, u32[]{:S(2)}) copy-start(f32[2133]{0:T(1024)} %param.29) | copy-start | bytes 25600
  586.8 68.8 %copy-start.28 = (f32[2133]{0:T(1024)S(1)}, f32[2133]{0:T(1024)}, u32[]{:S(2)}) copy-start(f32[2133]{0:T(1024)} %param.31) | copy-start | bytes 25600
  588.7 72.1 %slice-start = ((s8[5570560]{0:T(1024)(128)(4,1)}), s8[1376256]{0:T(1024)(128)(4,1)S(1)}, s32[]{:S(2)}) async-start(s8[5570560]{0:T(1024)(128)(4,1)} %bitcast.136), calls=%async_computation.9 | async-start | bytes 2752512
  659.3 3.4 collective-permute-start.7
  667.3 35.7 %collective-permute-start.6 = (f32[392,512]{1,0:T(8,128)S(1)}, f32[392,512]{1,0:T(8,128)S(1)}, u32[]{:S(2)}, u32[]{:S(2)}) collective-permute-start(f32[392,512]{1,0:T(8,128)S(1)} %dynamic-slice_bitcast_fusion.1), channel_id=1, source_target_pairs={{1,0},{0,1},{3,2},{2,3},{5,4},{4,5},{7,6},{6,7},{9,8},{8,9},{11,10... | collective-permute-start | bytes 2408456 | tf_op jit(solution)/shard_map/ppermute | solution.py:114
  814.4 41.0 %copy-start.9 = (f32[1024,85]{0,1:T(8,128)S(1)}, f32[1024,85]{0,1:T(8,128)}, u32[]{:S(2)}) copy-start(f32[1024,85]{0,1:T(8,128)} %all-reduce.5.cloned.1.call-done) | copy-start | bytes 1044484
  (35 other events, 158.0 us)
Sparse Core Ops, SparseCore 0:
  29.3 116.9 all-gather.10
  203.0 60.9 reduce-scatter.4
  268.7 248.9 reduce-scatter.2
Sparse Core Ops, SparseCore 1:
  233.8 61.3 all-gather.6
  301.8 257.0 all-reduce.4
  562.3 60.7 all-gather.8
  625.9 170.9 all-gather.12

commit v2 on v1

--- a/solution.py
+++ b/solution.py
@@ -1,4 +1,5 @@
 import functools
+import math
 
 import jax
 import jax.numpy as jnp
@@ -113,6 +114,282 @@
         part = lax.dynamic_index_in_dim(parts, target, 0, keepdims=False)
         got.append(lax.ppermute(part, "roi", [((i + shift) % members, i) for i in range(members)]))
     return in_order(got)
+
+
+def flip(index, bits):
+    value, bit = index, 1
+    while bit <= bits:
+        if bits & bit:
+            value = value + bit * (1 - 2 * (index // bit % 2))
+        bit *= 2
+    return value
+
+
+def piece_rows(rows):
+    return max(n for n in range(16, 257, 16) if rows % n == 0)
+
+
+def lowest_bit(value):
+    return (value & -value).bit_length() - 1
+
+
+SPLIT = (0, 0, 2, 2, 2)
+ORDERS = (
+    (1, 2, 0, 3, 4),
+    (1, 2, 0, 3, 4),
+    (1, 2, 3, 0, 4),
+    (1, 3, 2, 0, 4),
+    (0, 1, 2, 3, 4),
+    (3, 0, 1, 2, 4),
+    (3, 1, 2, 0, 4),
+)
+
+
+class SumPlan:
+    def __init__(self, groups):
+        self.groups = groups
+        self.stages = groups.bit_length() - 1
+        even = range(groups - 2, -1, -2)
+        self.order = [r for r in even if r % 4 == 2] + [r for r in even if r % 4 == 0]
+
+    def count(self, stage):
+        return self.groups >> (stage + 1)
+
+    def slot(self, stage, r):
+        return r >> (stage + 1)
+
+
+def sum_kernel(plan, arrays, *refs):
+    inputs = refs[:arrays]
+    outputs = refs[arrays : 3 * arrays]
+    rest = refs[3 * arrays :]
+    groups, stages = plan.groups, plan.stages
+    me = lax.axis_index("dp")
+    member = lax.axis_index("roi")
+    partners = [flip(me, 1 << stage) for stage in range(stages)]
+
+    barrier = pltpu.get_barrier_semaphore()
+    for partner in partners:
+        pl.semaphore_signal(
+            barrier, inc=1, device_id=(partner, member), device_id_type=pl.DeviceIdType.MESH
+        )
+    pl.semaphore_wait(barrier, stages)
+
+    per_array = 1 + 2 * stages - 1 + 5
+    parts = []
+    for a in range(arrays):
+        mine = rest[a * per_array : (a + 1) * per_array]
+        own, land, leave = mine[0], mine[1 : 1 + stages], (None,) + mine[1 + stages : 2 * stages]
+        parts.append((inputs[a], own, land, leave) + tuple(mine[2 * stages :]))
+
+    def near(a, r):
+        source, own, _, _, own_sem, *_ = parts[a]
+        slot = r >> 1
+        return pltpu.make_async_copy(source.at[flip(me, r)], own.at[slot], own_sem.at[slot])
+
+    def first_copy(a, r):
+        source, _, land, _, _, send0, recv0, _, _ = parts[a]
+        slot = r >> 1
+        return pltpu.make_async_remote_copy(
+            src_ref=source.at[flip(me, r)],
+            dst_ref=land[0].at[slot],
+            send_sem=send0.at[slot],
+            recv_sem=recv0.at[slot],
+            device_id=(partners[0], member),
+            device_id_type=pl.DeviceIdType.MESH,
+        )
+
+    def later_copy(a, stage, r, piece):
+        _, _, land, leave, _, _, _, send, recv = parts[a]
+        rows = piece_rows(land[0].shape[1])
+        slot = plan.slot(stage, r)
+        at = pl.ds(pl.multiple_of(piece * rows, 16), rows)
+        base = sum(plan.count(t) for t in range(1, stage)) + slot
+        return pltpu.make_async_remote_copy(
+            src_ref=leave[stage].at[slot, at],
+            dst_ref=land[stage].at[slot, at],
+            send_sem=send.at[base, piece],
+            recv_sem=recv.at[base, piece],
+            device_id=(partners[stage], member),
+            device_id_type=pl.DeviceIdType.MESH,
+        )
+
+    for r in plan.order:
+        for a in range(arrays):
+            first_copy(a, r + 1).start()
+        for a in range(arrays):
+            near(a, r).start()
+
+    def pieces(a):
+        rows = parts[a][2][0].shape[1]
+        return rows // piece_rows(rows)
+
+    for r in plan.order:
+        stage = lowest_bit(r) if r else stages
+        for a in range(arrays):
+            _, own, land, leave, *_ = parts[a]
+            near(a, r).wait()
+            first_copy(a, r).wait_recv()
+            rows = piece_rows(land[0].shape[1])
+
+            def step(piece, carry, a=a, own=own, land=land, leave=leave, rows=rows):
+                at = pl.ds(pl.multiple_of(piece * rows, 16), rows)
+                total = own[r >> 1, at].astype(jnp.float32) + land[0][r >> 1, at].astype(
+                    jnp.float32
+                )
+                for t in range(1, stage):
+                    later_copy(a, t, r, piece).wait_recv()
+                    total += land[t][plan.slot(t, r), at].astype(jnp.float32)
+                if r:
+                    leave[stage][plan.slot(stage, r), at] = total.astype(own.dtype)
+                    later_copy(a, stage, r, piece).start()
+                else:
+                    outputs[2 * a][at] = total
+                    outputs[2 * a + 1][at] = total.astype(own.dtype)
+                return carry
+
+            lax.fori_loop(0, pieces(a), step, 0)
+
+    for r in plan.order:
+        for a in range(arrays):
+            first_copy(a, r + 1).wait_send()
+            if r:
+                stage = lowest_bit(r)
+
+                def step(piece, carry, a=a, stage=stage, r=r):
+                    later_copy(a, stage, r, piece).wait_send()
+                    return carry
+
+                lax.fori_loop(0, pieces(a), step, 0)
+
+
+def sum_groups(*arrays):
+    groups = arrays[0].shape[0]
+    plan = SumPlan(groups)
+    out_shape, scratch = [], []
+    for array in arrays:
+        _, rows, width = array.shape
+        out_shape += [
+            jax.ShapeDtypeStruct((rows, width), jnp.float32),
+            jax.ShapeDtypeStruct((rows, width), array.dtype),
+        ]
+        half = groups // 2
+        block = (rows, width)
+        scratch += [pltpu.VMEM((half,) + block, array.dtype)]
+        scratch += [pltpu.VMEM((plan.count(t),) + block, array.dtype) for t in range(plan.stages)]
+        scratch += [
+            pltpu.VMEM((plan.count(t),) + block, array.dtype) for t in range(1, plan.stages)
+        ]
+        later = (half - 1, rows // piece_rows(rows))
+        scratch += [pltpu.SemaphoreType.DMA((half,))] * 3
+        scratch += [pltpu.SemaphoreType.DMA(later)] * 2
+    return pl.pallas_call(
+        functools.partial(sum_kernel, plan, len(arrays)),
+        in_specs=[pl.BlockSpec(memory_space=pl.ANY)] * len(arrays),
+        out_specs=[pl.BlockSpec(memory_space=pltpu.VMEM)] * len(out_shape),
+        out_shape=out_shape,
+        scratch_shapes=scratch,
+        compiler_params=pltpu.CompilerParams(
+            collective_id=0, has_side_effects=True, vmem_limit_bytes=56 * MIB
+        ),
+        name="sum_groups",
+    )(*arrays)
+
+
+def gather_kernel(arrays, plan, *refs):
+    inputs, outputs = refs[:arrays], refs[arrays : 2 * arrays]
+    own_sem, send, recv = refs[2 * arrays :]
+    axes = len(SPLIT)
+    sizes = outputs[0].shape[:axes]
+    dp = lax.axis_index("dp")
+    me = [lax.axis_index("roi")]
+    for axis in range(1, axes):
+        me.append(dp // math.prod(sizes[axis + 1 :]) % sizes[axis])
+    me = tuple(me)
+
+    def device(axis, shift):
+        spot = list(me)
+        spot[axis] = (me[axis] + shift) % sizes[axis]
+        group = spot[1]
+        for other in range(2, axes):
+            group = group * sizes[other] + spot[other]
+        return (group, spot[0])
+
+    barrier = pltpu.get_barrier_semaphore()
+    peers = [(axis, shift) for axis in range(axes) for shift in range(1, sizes[axis])]
+    for axis, shift in peers:
+        pl.semaphore_signal(
+            barrier, inc=1, device_id=device(axis, shift), device_id_type=pl.DeviceIdType.MESH
+        )
+    pl.semaphore_wait(barrier, len(peers))
+
+    def copies(number, stage):
+        array, first, rows, order = plan[number]
+        done, axis = order[:stage], order[stage]
+        held = tuple(slice(None) if d in done else me[d] for d in range(axes))
+        at = pl.ds(first, rows)
+        region = outputs[array].at[held + (at,)]
+        source = inputs[array].at[at] if stage == 0 else region
+        before = sum(sizes[d] - 1 for d in done)
+        return [
+            pltpu.make_async_remote_copy(
+                src_ref=source,
+                dst_ref=region,
+                send_sem=send.at[number, before + shift - 1],
+                recv_sem=recv.at[number, before + shift - 1],
+                device_id=device(axis, shift),
+                device_id_type=pl.DeviceIdType.MESH,
+            )
+            for shift in range(1, sizes[axis])
+        ]
+
+    for number in range(len(plan)):
+        for copy in copies(number, 0):
+            copy.start()
+    own = [
+        pltpu.make_async_copy(inputs[a], outputs[a].at[me], own_sem.at[a]) for a in range(arrays)
+    ]
+    for copy in own:
+        copy.start()
+    for copy in own:
+        copy.wait()
+    for stage in range(1, axes + 1):
+        for number in range(len(plan)):
+            for copy in copies(number, stage - 1):
+                copy.wait_recv()
+            if stage < axes:
+                for copy in copies(number, stage):
+                    copy.start()
+    for stage in range(axes):
+        for number in range(len(plan)):
+            for copy in copies(number, stage):
+                copy.wait_send()
+
+
+def gather_all(*arrays):
+    members = lax.axis_size("roi")
+    groups = lax.axis_size("dp")
+    sizes = (members, groups // math.prod(SPLIT[2:])) + SPLIT[2:]
+    plan = []
+    for a, array in enumerate(arrays):
+        rows = array.shape[0]
+        step = piece_rows(rows)
+        for n, first in enumerate(range(0, rows, step)):
+            plan.append((a, first, step, ORDERS[n % len(ORDERS)]))
+    copies = sum(size - 1 for size in sizes)
+    return pl.pallas_call(
+        functools.partial(gather_kernel, len(arrays), plan),
+        in_specs=[pl.BlockSpec(memory_space=pl.ANY)] * len(arrays),
+        out_specs=[pl.BlockSpec(memory_space=pl.ANY)] * len(arrays),
+        out_shape=[jax.ShapeDtypeStruct(sizes + array.shape, array.dtype) for array in arrays],
+        scratch_shapes=[
+            pltpu.SemaphoreType.DMA((len(arrays),)),
+            pltpu.SemaphoreType.DMA((len(plan), copies)),
+            pltpu.SemaphoreType.DMA((len(plan), copies)),
+        ],
+        compiler_params=pltpu.CompilerParams(collective_id=1, has_side_effects=True),
+        name="gather_all",
+    )(*arrays)
 
 
 def lane_coordinates(rows, first_lane, lanes):
@@ -297,6 +574,19 @@
     )(fine, coarse, lane_places, grads)
 
 
+def split(value):
+    high = value.astype(jnp.bfloat16)
+    return high, (value - high.astype(jnp.float32)).astype(jnp.bfloat16)
+
+
+def split_dot(left_side, right_side):
+    high, low = split(left_side)
+    other_high, other_low = split(right_side)
+    product = jnp.dot(high, other_low, preferred_element_type=jnp.float32)
+    product += jnp.dot(low, other_high, preferred_element_type=jnp.float32)
+    return product + jnp.dot(high, other_high, preferred_element_type=jnp.float32)
+
+
 def shampoo_kernel(left_ref, root_ref, full_ref, own_ref, right_root_ref, weight_ref,
                    new_left_ref, new_weight_ref, mixed, *, rate):
     step = pl.program_id(0)
@@ -318,11 +608,7 @@
 
     @pl.when(step == pl.num_programs(0) - 1)
     def _():
-        value = mixed[...]
-        high = value.astype(jnp.bfloat16)
-        low = (value - high.astype(jnp.float32)).astype(jnp.bfloat16)
-        update = jnp.dot(high, right_root_ref[...], preferred_element_type=jnp.float32)
-        update += jnp.dot(low, right_root_ref[...], preferred_element_type=jnp.float32)
+        update = split_dot(mixed[...], right_root_ref[...])
         new_weight_ref[...] = weight_ref[...] - rate * update
 
 
@@ -419,6 +705,10 @@
         axis=0,
     )
     gathered = lax.all_gather(payload, "dp", axis=0)
+    right_roots, gathered = lax.optimization_barrier(
+        (jnp.stack([right_first_root, right_second_root]), gathered)
+    )
+    right_roots = lax.all_gather(right_roots, ("dp", "roi"), axis=1, tiled=True)
     first_half = gathered[:, : members * owned].reshape(features, width)
     second_full = gathered[:, members * owned :].reshape(hidden, hidden)
 
@@ -511,20 +801,14 @@
     grad_first = (rows_by_rows(group_second, second_rows) * silu_slope(first_pre)).astype(
         jnp.bfloat16
     )
-    first_term = cols_by_cols(pooled, grad_first)
-    second_term = cols_by_cols(first_act, group_second)
-    first_sum = lax.psum_scatter(first_term, "dp", scatter_dimension=0, tiled=True)
-    second_sum = lax.psum_scatter(second_term, "dp", scatter_dimension=0, tiled=True)
-
-    grad_pooled = rows_by_rows(grad_first, first_half).astype(jnp.bfloat16)
-    map_partial = unpool(fine, coarse, lane_places, grad_pooled, images, cells, channels)
-    map_parts = map_partial.reshape(images, members, cells // members, channels)
-    map_parts = jnp.swapaxes(map_parts, 0, 1)
-    map_own = lax.dynamic_index_in_dim(map_parts, me, 0, keepdims=False)
-    map_traded = trade_members(map_parts.astype(jnp.bfloat16)).astype(jnp.float32)
-    keep = (jnp.arange(members) == me)[:, None, None, None]
-    map_gradient = map_own + jnp.sum(jnp.where(keep, 0.0, map_traded), axis=0)
-
+    first_term = cols_by_cols(pooled, grad_first).astype(jnp.bfloat16)
+    second_term = cols_by_cols(first_act, group_second).astype(jnp.bfloat16)
+    block = features // groups
+    padding = round_up(block, 16) - block
+    first_term = first_term.reshape(groups, block, width)
+    if padding:
+        first_term = jnp.pad(first_term, ((0, 0), (0, padding), (0, 0)))
+    second_term = second_term.reshape(groups, -1, width)
     zeros = jnp.zeros((hidden,), jnp.float32)
     bias_term = jnp.concatenate(
         [
@@ -535,24 +819,43 @@
             jnp.sum(grad_out, axis=0, dtype=jnp.float32),
         ]
     )
-    head_gradient, bias_gradient = lax.psum((head_term, bias_term), ("dp", "roi"))
-
-    first_gradient = trade_members(first_sum.reshape(members, owned, width))
+    small_rows = round_up(hidden + (biases.shape[0] + 127) // 128, 16 * groups)
+    bias_space = (small_rows - hidden) * 128
+    small_term = jnp.concatenate(
+        [
+            jnp.pad(head_term, ((0, 0), (0, 128 - outs))),
+            jnp.pad(bias_term, (0, bias_space - bias_term.shape[0])).reshape(-1, 128),
+        ],
+        axis=0,
+    ).reshape(groups, small_rows // groups, 128)
+    first_sum, first_sum_low, second_sum, second_sum_low, small_sum, _ = sum_groups(
+        first_term, second_term, small_term
+    )
+
+    grad_pooled = rows_by_rows(grad_first, first_half).astype(jnp.bfloat16)
+    map_partial = unpool(fine, coarse, lane_places, grad_pooled, images, cells, channels)
+    map_parts = map_partial.reshape(images, members, cells // members, channels)
+    map_parts = jnp.swapaxes(map_parts, 0, 1)
+    map_own = lax.dynamic_index_in_dim(map_parts, me, 0, keepdims=False)
+    map_traded = trade_members(map_parts.astype(jnp.bfloat16)).astype(jnp.float32)
+    keep = (jnp.arange(members) == me)[:, None, None, None]
+    map_gradient = map_own + jnp.sum(jnp.where(keep, 0.0, map_traded), axis=0)
+
+    first_gradient = trade_members(first_sum[:block].reshape(members, owned, width))
     first_gradient = jnp.swapaxes(first_gradient, 0, 1).reshape(owned, hidden)
     devices = groups * members
     second_gradient = lax.ppermute(
-        second_sum,
+        second_sum.reshape(owned_second, hidden),
         ("dp", "roi"),
         [((b % groups) * members + b // groups, b) for b in range(devices)],
     )
-    first_reduced = lax.all_gather(first_sum.astype(jnp.bfloat16), ("roi", "dp"), axis=0)
-    first_reduced = first_reduced.reshape(members, features, width)
-    second_reduced = lax.all_gather(
-        second_sum.astype(jnp.bfloat16), ("roi", "dp"), axis=0, tiled=True
-    )
-    right_roots = jnp.stack([right_first_root, right_second_root]).astype(jnp.bfloat16)
-    right_roots = lax.all_gather(right_roots, ("dp", "roi"), axis=1, tiled=True)
-
+    first_reduced, second_reduced, small = gather_all(first_sum_low, second_sum_low, small_sum)
+    small = jnp.sum(small.reshape(members, small_rows, 128), axis=0)
+    head_gradient = small[:hidden, :outs]
+    bias_gradient = small[hidden:].reshape(-1)[: biases.shape[0]]
+    first_reduced = first_reduced.reshape(members, groups, block + padding, width)
+    first_reduced = first_reduced[:, :, :block].reshape(members, features, width)
+    second_reduced = second_reduced.reshape(hidden, hidden)
     own_first = lax.dynamic_slice_in_dim(first_reduced, owner * owned, owned, 1)
     new_left_first, new_first_weight = shampoo(
         left_first, left_first_root, first_reduced, own_first, right_roots[0], first_weight,
@@ -577,11 +880,7 @@
     mixed = jnp.dot(
         left_second_root.astype(jnp.bfloat16), second_reduced, preferred_element_type=jnp.float32
     )
-    mixed_high = mixed.astype(jnp.bfloat16)
-    mixed_low = (mixed - mixed_high.astype(jnp.float32)).astype(jnp.bfloat16)
-    update = jnp.dot(mixed_high, right_roots[1], preferred_element_type=jnp.float32) + jnp.dot(
-        mixed_low, right_roots[1], preferred_element_type=jnp.float32
-    )
+    update = split_dot(mixed, right_roots[1])
     new_second_weight = second_weight - RATE_SECOND * update
 
     new_head_moment, new_head_weight = diagonal_step(

time: 869 us -> 646 us (0.74)
  waiting for transfers between devices: 489 us -> 85.3 us
  Pallas kernels: 120 us -> 369 us
  blocking collectives: 64.4 us -> 0 us
  local copies, waits for them, and re-layouts: 34.3 us -> 59.3 us
  matrix products: 90.5 us -> 74.4 us
  starting transfers between devices: 21.7 us -> 11.4 us
    reduce_scatter x2 -> x0, waiting for transfers between devices: 284 us -> none  [the longest x1 252 us: local(): lax.psum_scatter(first_term, 'dp', scatter_dimension=0, tiled=True)]
    pallas_call x0 -> x2, Pallas kernels: none -> 246 us  [the longest x1 154 us: gather_all(): pl.pallas_call(functools.partial(gather_kernel, len(arrays), plan), in_sp...]
    all_gather x2 -> x0, waiting for transfers between devices: 89.4 us -> none  [the longest x1 89.4 us: local(): lax.all_gather(first_sum.astype(jnp.bfloat16), ('roi', 'dp'), axis=0)]
    psum x1 -> x0, blocking collectives: 64.4 us -> none  [local(): lax.psum((head_term, bias_term), ('dp', 'roi'))]
    ppermute x4, waiting for transfers between devices: 37.5 us -> 13.3 us  [trade_members(): lax.ppermute(part, 'roi', [((i + shift) % members, i) for i in range(memb...]
    slice x0 -> x1, local copies, waits for them, and re-layouts: none -> 10 us  [local(): first_reduced[member]]
  transfers between devices with their start and end apart: 15 -> 10, of which waited for: 8 -> 4; matrix products, arithmetic and copies ran while one was open for 10% -> 18% of each run, Pallas kernels for 9% -> 51%
where the time goes in v2:
time: 646 us; the launch traced here: 637 us
  Pallas kernels  369 us (57%)
  waiting for transfers between devices  85.3 us (13%)
  matrix products  74.4 us (12%)
  local copies, waits for them, and re-layouts  59.3 us (9%)
  other arithmetic  22.8 us (4%)
  between operations  15.2 us (2%)
  starting transfers between devices  11.4 us (2%)
    pallas_call x1, Pallas kernels, gather_all(): pl.pallas_call(functools.partial(gather_kernel, len(arrays), plan), in_sp...  154 us
    pallas_call x1, Pallas kernels, sum_groups(): pl.pallas_call(functools.partial(sum_kernel, plan, len(arrays)), in_specs...  91.9 us
    all_gather x1, waiting for transfers between devices, local(): gathered = lax.all_gather(payload, 'dp', axis=0)  60.1 us
    pallas_call x1, Pallas kernels, pool(): pl.pallas_call(pool_kernel, grid_spec=pltpu.PrefetchScalarGridSpec(num_sc...  45.8 us
    pallas_call x1, Pallas kernels, shampoo(): pl.pallas_call(functools.partial(shampoo_kernel, rate=rate), grid=(order...  41.7 us
    pallas_call x1, Pallas kernels, unpool(): pl.pallas_call(functools.partial(unpool_kernel, tiles=tiles), grid_spec=p...  35.1 us
    dot_general x6, matrix products, cols_by_cols(): lax.dot_general(left_side, right_side, (((0,), (0,)), ((), ())), preferre...  32.9 us
    dot_general x4, matrix products, rows_by_rows(): lax.dot_general(left_side, right_side, (((1,), (1,)), ((), ())), preferre...  19.2 us
  transfers between devices with their start and end apart: 10, of which 4 were waited for; matrix products, arithmetic and copies ran while one was open for 18% of the time, Pallas kernels for 51%

profile of v2, /device:TPU:0, one launch (start us, length us, event | category | flops | bytes accessed | tf_op | source)
XLA Modules:
  0.0 637.2 jit_solution(3232946141238700491)
XLA Ops:
  9.5 2.9 fusion.23
  12.5 3.0 collective-permute-start.1
  15.5 10.7 %collective-permute-done.1 = bf16[456,512]{1,0:T(8,128)(2,1)S(1)} collective-permute-done((bf16[456,512]{1,0:T(8,128)(2,1)S(1)}, bf16[456,512]{1,0:T(8,128)(2,1)S(1)}, u32[]{:S(2)}, u32[]{:S(2)}) %collective-permute-start.1) | collective-permute-done | bytes 466976 | tf_op jit(solution)/shard_map/ppermute | solution.py:115
  39.0 45.8 %pool.1 = bf16[576,12544]{1,0:T(8,128)(2,1)} custom-call(s32[36]{0:T(128)S(1)} %reduce_max.27.fine_ref, s32[36]{0:T(128)S(1)} %reduce_max.28.coarse_ref, f32[576,128]{1,0:T(8,128)S(1)} %pad.20.place_ref, bf16[4,1408,256]{2,1,0:T(8,128)(2,1)S(1)} %pad.21.maps_ref), custom_call_target="tpu_custom_call" | custom-call | flops 14797504512 | bytes 14450688 | tf_op jit(solution)/shard_map/pool/pallas_call | solution.py:477
  84.8 60.1 %all-gather.6.cloned.1.call-done = bf16[14592,512]{1,0:T(8,128)(2,1)} async-done(((bf16[912,512]{1,0:T(8,128)(2,1)}), bf16[14592,512]{1,0:T(8,128)(2,1)}) %all-gather.6.cloned.1.call-update) | async-done | bytes 14942224 | tf_op jit(solution)/shard_map/all_gather | solution.py:707
  144.9 6.4 slice.143
  151.3 16.4 %multiply_convert_fusion.1 = (bf16[576,512]{1,0:T(8,128)(2,1)S(1)}, f32[576,512]{1,0:T(8,128)}) fusion(f32[512]{0:T(512)S(1)} %dynamic_slice.53, bf16[576,12544]{1,0:T(8,128)(2,1)} %pool.1, bf16[12544,512]{1,0:T(8,128)(2,1)S(1)} %bitcast.171), kind=kOutput, calls=%fused_computation.40 | convolution fusion | flops 7400521728 | bytes 29067264 | tf_op jit(solution)/shard_map/dot_general | solution.py:766
  175.4 2.6 collective-permute-done.2
  188.2 11.9 %collective-permute-done.4 = bf16[288,1024]{1,0:T(8,128)(2,1)S(1)} collective-permute-done((bf16[288,1024]{1,0:T(8,128)(2,1)S(1)}, bf16[288,1024]{1,0:T(8,128)(2,1)S(1)}, u32[]{:S(2)}, u32[]{:S(2)}) %collective-permute-start.4) | collective-permute-done | bytes 589856 | tf_op jit(solution)/shard_map/ppermute | solution.py:104
  203.7 3.1 convolution_convert_fusion.2
  206.8 2.2 reshape.216.refs_1_
  209.0 18.7 %convolution_convert_fusion.1 = bf16[12544,512]{1,0:T(8,128)(2,1)} fusion(bf16[576,12544]{1,0:T(8,128)(2,1)} %pool.1, bf16[576,512]{1,0:T(8,128)(2,1)S(1)} %copy-done.34), kind=kOutput, calls=%fused_computation.1 | convolution fusion | flops 7405174784 | bytes 27885568 | tf_op jit(solution)/shard_map/dot_general | solution.py:80
  227.6 91.9 %sum_groups.1 = (f32[784,512]{1,0:T(8,128)}, bf16[784,512]{1,0:T(8,128)(2,1)}, f32[64,512]{1,0:T(8,128)}, bf16[64,512]{1,0:T(8,128)(2,1)}, f32[80,128]{1,0:T(8,128)}, /*index=5*/f32[80,128]{1,0:T(8,128)}) custom-call(bf16[16,784,512]{2,1,0:T(8,128)(2,1)} %bitcast.170, bf16[16,64,512]{2,1,0:T(8,128)(2,1)} %reshape.216.refs_1_, f32[16,80,128]{2,1,0:T(8,128)} %bitcast.177), custom_call_target="tpu_custom_call" | custom-call | tf_op jit(solution)/shard_map/sum_groups/pallas_call | solution.py:286
  319.5 154.4 %gather_all.1 = (bf16[2,2,2,2,2,784,512]{6,5,4,3,2,1,0:T(8,128)(2,1)}, bf16[2,2,2,2,2,64,512]{6,5,4,3,2,1,0:T(8,128)(2,1)}, f32[2,2,2,2,2,80,128]{6,5,4,3,2,1,0:T(8,128)}) custom-call(bf16[784,512]{1,0:T(8,128)(2,1)} %get-tuple-element.31.refs_0_, bf16[64,512]{1,0:T(8,128)(2,1)} %get-tuple-element.32.refs_1_, f32[80,128]{1,0:T(8,128)} %get-tuple-element.33.refs_2_), custom_call_target="tpu_custom_call" | custom-call | tf_op jit(solution)/shard_map/gather_all/pallas_call | solution.py:380
  474.0 2.7 reshape.222
  476.6 2.3 reduce_sum.94
  482.5 14.0 %convolution_convert_fusion.grad_ref = bf16[576,12544]{1,0:T(8,128)(2,1)} fusion(bf16[576,512]{1,0:T(8,128)(2,1)} %get-tuple-element.169, bf16[12544,512]{1,0:T(8,128)(2,1)} %bitcast.172), kind=kOutput, calls=%fused_computation | convolution fusion | flops 7405977600 | bytes 27885568 | tf_op jit(solution)/shard_map/dot_general | solution.py:74
  496.5 35.1 %unpool.1 = f32[4,1360,256]{2,1,0:T(8,128)S(1)} custom-call(s32[36]{0:T(128)S(1)} %reduce_max.27.fine_ref, s32[36]{0:T(128)S(1)} %reduce_max.28.coarse_ref, f32[36,8,896]{2,1,0:T(8,128)S(1)} %pad.22.place_ref, bf16[576,12544]{1,0:T(8,128)(2,1)} %convolution_convert_fusion.grad_ref), custom_call_target="tpu_custom_call" | custom-call | flops 7398752256 | bytes 14450688 | tf_op jit(solution)/shard_map/unpool/pallas_call | solution.py:551
  538.1 10.0 %fusion.91 = (bf16[1,2,2,2,2,784,512]{6,5,4,3,2,1,0:T(8,128)(2,1)S(1)}, bf16[1,2,2,2,2,784,512]{6,5,4,3,2,1,0:T(8,128)(2,1)S(1)}) fusion(bf16[2,2,2,2,2,784,512]{6,5,4,3,2,1,0:T(8,128)(2,1)} %get-tuple-element.34), kind=kLoop, calls=%fused_computation.199 | loop fusion | bytes 51380224 | tf_op jit(solution)/shard_map/slice | solution.py:870
  548.2 4.8 fusion.3
  553.0 4.8 fusion.1
  575.4 2.2 fusion.11
  580.4 4.9 slice_bitcast_fusion.1.right_root_ref
  585.3 41.7 %shampoo.1 = (f32[392,12544]{1,0:T(8,128)}, f32[392,1024]{1,0:T(8,128)}) custom-call(f32[392,12544]{1,0:T(8,128)} %left_ref.1, f32[392,12544]{1,0:T(8,128)} %root_ref.1, bf16[2,12544,512]{2,1,0:T(8,128)(2,1)} %bitcast.165, bf16[2,392,512]{2,1,0:T(8,128)(2,1)S(1)} %constant_dynamic-slice_fusion.1.own_ref, f32[1024,1024]{1,0:T(8,128)} %slice_bitcast_fusion.1.right_root_ref, ...), custom_call_target="tpu_custom_call" | custom-call | flops 20141047808 | bytes 84697088 | tf_op jit(solution)/shard_map/shampoo/pallas_call | solution.py:619
  (219 shorter events, 69.6 us)
Async XLA Ops:
  7.2 137.7 %all-gather.6.cloned.1.call-start = ((), (), s32[]{:S(2)}) async-start(), calls=%async_computation.1 | async-start | bytes 15876096 | tf_op jit(solution)/shard_map/all_gather | solution.py:707
  12.5 13.7 %collective-permute-start.1 = (bf16[456,512]{1,0:T(8,128)(2,1)S(1)}, bf16[456,512]{1,0:T(8,128)(2,1)S(1)}, u32[]{:S(2)}, u32[]{:S(2)}) collective-permute-start(bf16[456,512]{1,0:T(8,128)(2,1)S(1)} %bitcast.190), channel_id=1, source_target_pairs={{1,0},{0,1},{3,2},{2,3},{5,4},{4,5},{7,6},{6,7},{9,8},{8,9},{11,10... | collective-permute-start | bytes 1400840 | tf_op jit(solution)/shard_map/ppermute | solution.py:115
  26.5 5.4 copy-start.11
  27.5 552.8 %all-gather.4.cloned.1.call-start = ((), (), s32[]{:S(2)}) async-start(), calls=%async_computation | async-start | bytes 8650752 | tf_op jit(solution)/shard_map/all_gather | solution.py:711
  27.7 7.2 %collective-permute-start = (f32[288,11]{0,1:T(8,128)S(1)}, f32[288,11]{0,1:T(8,128)S(1)}, u32[]{:S(2)}, u32[]{:S(2)}) collective-permute-start(f32[288,11]{0,1:T(8,128)S(1)} %pad_maximum_fusion.9), channel_id=1, source_target_pairs={{1,0},{0,1},{3,2},{2,3},{5,4},{4,5},{7,6},{6,7},{9,8},{8,9},{11,10... | collective-permute-start | bytes 38024 | tf_op jit(solution)/shard_map/ppermute | solution.py:104
  151.3 16.4 %copy-start.2 = (bf16[16,784,512]{2,1,0:T(8,128)(2,1)}, bf16[16,784,512]{2,1,0:T(8,128)(2,1)S(1)}, u32[]{:S(2)}) copy-start(bf16[16,784,512]{2,1,0:T(8,128)(2,1)S(1)} %slice.143) | copy-start | bytes 38535172
  168.5 9.5 %collective-permute-start.2 = (bf16[288,512]{1,0:T(8,128)(2,1)}, bf16[288,512]{1,0:T(8,128)(2,1)}, u32[]{:S(2)}, u32[]{:S(2)}) collective-permute-start(bf16[288,512]{1,0:T(8,128)(2,1)} %dynamic-slice_bitcast_fusion.2), channel_id=1, source_target_pairs={{1,0},{0,1},{3,2},{2,3},{5,4},{4,5},{7,6},{6,7},{9,8},{8,9},{11,10... | collective-permute-start | bytes 884744 | tf_op jit(solution)/shard_map/ppermute | solution.py:115
  182.0 4.4 collective-permute-start.3
  185.6 14.5 %collective-permute-start.4 = (bf16[288,1024]{1,0:T(8,128)(2,1)S(1)}, bf16[288,1024]{1,0:T(8,128)(2,1)S(1)}, u32[]{:S(2)}, u32[]{:S(2)}) collective-permute-start(bf16[288,1024]{1,0:T(8,128)(2,1)S(1)} %get-tuple-element.167), channel_id=1, source_target_pairs={{1,0},{0,1},{3,2},{2,3},{5,4},{4,5},{7,6},{6,7},{9,8},{8,9},{11,10... | collective-permute-start | bytes 1769480 | tf_op jit(solution)/shard_map/ppermute | solution.py:104
  188.2 12.1 %copy-start.7 = (bf16[1024,1024]{1,0:T(8,128)(2,1)S(1)}, bf16[1024,1024]{1,0:T(8,128)(2,1)}, u32[]{:S(2)}) copy-start(bf16[1024,1024]{1,0:T(8,128)(2,1)} %reshape.209) | copy-start | bytes 6291460
  188.2 12.1 %copy-start.33 = (f32[576,512]{1,0:T(8,128)S(1)}, f32[576,512]{1,0:T(8,128)}, u32[]{:S(2)}) copy-start(f32[576,512]{1,0:T(8,128)} %get-tuple-element.163) | copy-start | bytes 3538948
  203.7 5.3 copy-start.34
  481.0 87.8 %collective-permute-start.6 = (f32[392,512]{1,0:T(8,128)}, f32[392,512]{1,0:T(8,128)}, u32[]{:S(2)}, u32[]{:S(2)}) collective-permute-start(f32[392,512]{1,0:T(8,128)} %dynamic-slice_bitcast_fusion.1), channel_id=1, source_target_pairs={{1,0},{0,1},{3,2},{2,3},{5,4},{4,5},{7,6},{6,7},{9,8},{8,9},{11,10... | collective-permute-start | bytes 2408456 | tf_op jit(solution)/shard_map/ppermute | solution.py:115
  535.3 39.3 %collective-permute-start.5 = (bf16[4,680,256]{2,1,0:T(8,128)(2,1)}, bf16[4,680,256]{2,1,0:T(8,128)(2,1)}, u32[]{:S(2)}, u32[]{:S(2)}) collective-permute-start(bf16[4,680,256]{2,1,0:T(8,128)(2,1)} %dynamic-slice_bitcast_fusion), channel_id=1, source_target_pairs={{1,0},{0,1},{3,2},{2,3},{5,4},{4,5},{7,6},{6,7},{9,8},{8,9},{11,10... | collective-permute-start | bytes 4177928 | tf_op jit(solution)/shard_map/ppermute | solution.py:115
  552.9 5.5 copy-start.25
  552.9 5.5 copy-start.27
  557.7 6.3 copy-start.21
  557.7 7.2 %copy-start.19 = (f32[32,1024]{1,0:T(8,128)S(1)}, f32[32,1024]{1,0:T(8,128)}, u32[]{:S(2)}) copy-start(f32[32,1024]{1,0:T(8,128)} %param.38) | copy-start | bytes 393220
  561.1 5.2 copy-start.20
  564.1 4.7 collective-permute-start.7
  573.1 5.4 slice-start
  580.4 5.0 copy-start.1
  580.4 46.6 %slice-start.2 = ((s8[8388608]{0:T(1024)(128)(4,1)}), s8[4194304]{0:T(1024)(128)(4,1)S(1)}, s32[]{:S(2)}) async-start(s8[8388608]{0:T(1024)(128)(4,1)} %bitcast.166), calls=%async_computation.4 | async-start | bytes 8388608
  585.3 41.7 %slice-start.3 = ((s8[8388608]{0:T(1024)(128)(4,1)}), s8[4194304]{0:T(1024)(128)(4,1)S(1)}, s32[]{:S(2)}) async-start(s8[8388608]{0:T(1024)(128)(4,1)} %bitcast.166), calls=%async_computation.5 | async-start | bytes 8388608
  (27 other events, 69.0 us)
Sparse Core Ops, SparseCore 0:
  27.7 117.2 all-gather.5
  175.5 84.3 all-gather.3
